TPU v7x, 32 devices: a whole 2x2x4 slice. The times are simulated.
32 devices in a mesh: section: 2 (over x), rep: 16 (over z, y, core).
Axes of the slice: x: 2, y: 2, z: 4, core: 2. Of those that a mesh axis runs over, the one named last changes fastest.
Arguments:
- ends_in: bfloat16 [2, 8192, 768], P('section', 'rep'), may hold values from -6 to 6
- lengths: int32 [16, 2, 4], P('rep'), may hold values from 0 to 256, as said below
- times: int32 [16, 2, 4], P('rep'), may hold values from 0 to 999
- norm_gain: bfloat16 [2, 768], P('section'), may hold values from 0.099609375 to 1.8984375
- attend_in: bfloat16 [2, 768, 2304], P('section'), may hold values from -0.21875 to 0.21875
- attend_out: bfloat16 [2, 768, 768], P('section'), may hold values from -1.25 to 1.25
- time_weight: bfloat16 [2, 128, 2304], P('section'), may hold values from -0.5 to 0.5
- time_bias: bfloat16 [2, 2304], P('section'), may hold values from -3 to 3
- expand_weight: bfloat16 [2, 768, 3072], P('section'), may hold values from -0.21875 to 0.21875
- expand_bias: bfloat16 [2, 3072], P('section'), may hold values from -3 to 3
- reduce_weight: bfloat16 [2, 3072, 768], P('section'), may hold values from -0.109375 to 0.109375
- reduce_bias: bfloat16 [2, 768], P('section'), may hold values from -3 to 3
Outputs:
- ends_out: bfloat16 [2, 8192, 768], P('section', 'rep')
- grad_norm_gain: float32 [2, 768], P('section', 'rep')
- grad_attend_in: float32 [2, 768, 2304], P('section', 'rep')
- grad_attend_out: float32 [2, 768, 768], P('section', 'rep')
- grad_time_weight: float32 [2, 128, 2304], P('section', 'rep')
- grad_time_bias: float32 [2, 2304], P('section', 'rep')
- grad_expand_weight: float32 [2, 768, 3072], P('section', 'rep')
- grad_expand_bias: float32 [2, 3072], P('section', 'rep')
- grad_reduce_weight: float32 [2, 3072, 768], P('section', 'rep')
- grad_reduce_bias: float32 [2, 768], P('section', 'rep')
Inputs may be any that keep to these rules, and one draw needn't show every extreme that they name: Each micro-batch's 4 lengths sum to 256: either one sequence of 256 tokens followed by zeros, or 4 sequences of 64 tokens; some micro-batch of some replica holds one sequence.
All inputs are finite; a program needn't handle non-finite values.
Results may differ from a plain program's by a relative error of at most 0.019.
Values may be sent and summed in bfloat16 or wider, within the bound.
No kernel may reach another device: no remote copies, remote signals or barrier semaphores. Data moves between devices by JAX's collectives and lax.ppermute only.
A program may use at most 192 MiB of HBM per device.

v0:
```python
from functools import partial
import inspect
import math

import jax
import jax.numpy as jnp
import numpy as np
from jax import lax
from jax.experimental import pallas as pl
from jax.experimental.pallas import tpu as pltpu
from jax.sharding import PartitionSpec as P

HEADS = 12
HEAD = 64
EMB = 128
SEGS = 4
ANY = pl.ANY
VMEM = pltpu.MemorySpace.VMEM
SMEM = pltpu.MemorySpace.SMEM
F32 = jnp.float32
BF16 = jnp.bfloat16
ROOT_HALF = 0.7071067811865476
ROOT_TAU = 0.3989422804014327
TILE = 384
SMALL_ROWS = 8
GAIN_ROWS = 16


class Bag(dict):
    __getattr__ = dict.__getitem__


def dot(left, right, left_dim=1, right_dim=0):
    return lax.dot_general(
        left, right, (((left_dim,), (right_dim,)), ((), ())), preferred_element_type=F32
    )


def repeat(count, body):
    for i in range(count):
        body(i)


def steps_of(count, size, body):
    def several(i, _):
        for j in range(size):
            body(size * i + j)
        return _

    lax.fori_loop(0, count // size, several, 0)


def lanes(index, size, start=0):
    if isinstance(index, int):
        return slice(start + index * size, start + (index + 1) * size)
    return pl.ds(pl.multiple_of(start + index * size, size), size)


def swap_halves(values, low_half):
    forth = pltpu.roll(values, 128 - HEAD // 2, 1)
    back = pltpu.roll(values, HEAD // 2, 1)
    return jnp.where(low_half, forth, back)


def norm_parts(values):
    center = values - jnp.mean(values, axis=-1, keepdims=True)
    spread = jnp.mean(center * center, axis=-1, keepdims=True)
    factor = lax.rsqrt(spread + 1e-05)
    return center * factor, factor


def norm_back(grad, unit, factor):
    return factor * (
        grad
        - jnp.mean(grad, axis=-1, keepdims=True)
        - unit * jnp.mean(grad * unit, axis=-1, keepdims=True)
    )


class Held:
    def __init__(self, bufs, loads, stores, sems):
        self.bufs = bufs
        self.loads = loads
        self.stores = stores
        self.sems = sems
        self.names = {id(buf): name for name, buf in bufs.items()}
        self.spots = {name: n for n, name in enumerate(loads)}
        self.pending = set(loads)
        self.waiting = set(loads)
        self.leaving = {}

    def load(self, name):
        return pltpu.make_async_copy(
            self.loads[name], self.bufs[name], self.sems.at[self.spots[name]]
        )

    def store(self, name, at):
        number, _ = self.leaving[(name, at)]
        source, target = self.bufs[name], self.stores[name]
        if at is not None:
            spot = tuple(pl.ds(*item) for item in at)
            source, target = source.at[spot], target.at[spot]
        return pltpu.make_async_copy(source, target, self.sems.at[number])

    def begin(self, *bufs):
        for buf in bufs:
            name = self.names[id(buf)]
            if name in self.waiting:
                self.waiting.remove(name)
                self.load(name).start()

    def begin_all(self):
        self.begin(*[self.bufs[name] for name in self.loads])

    def need(self, *bufs):
        self.begin(*bufs)
        for buf in bufs:
            name = self.names[id(buf)]
            if name in self.pending:
                self.pending.remove(name)
                self.load(name).wait()

    def done(self, *bufs, at=None):
        for buf in bufs:
            name = self.names[id(buf)]
            if name in self.stores:
                self.leaving[(name, at)] = (len(self.loads) + len(self.leaving), at)
                self.store(name, at).start()

    def finish(self):
        for name, at in self.leaving:
            self.store(name, at).wait()


class Layer:
    def __init__(self, sizes, slot, refs):
        self.span, self.width, self.hidden, self.count = sizes
        self.slot = slot
        (
            lengths, section, core, self.mods, self.trig, self.embed, self.gain, self.ebias,
            self.rbias,
        ) = refs
        self.section = section[0]
        self.low = core[0] == 0
        self.single = lengths[slot, 0] == self.span
        self.pairs = self.width // 128
        self.seg = self.span // SEGS
        self.step = 1024
        self.tiles = self.hidden // self.step
        place = lax.broadcasted_iota(jnp.int32, (self.span, 128), 1)
        self.low_half = place % HEAD < HEAD // 2
        self.low_head = place < HEAD
        row = lax.broadcasted_iota(jnp.int32, (1, 128), 1) // HEAD
        self.head_row = [(row == i).astype(F32).astype(BF16) for i in range(2)]
        self.blocks = [(b, slice(b * self.seg, (b + 1) * self.seg)) for b in range(SEGS)]

    def trig_pair(self):
        cos_all, sin_all = self.trig[0], self.trig[1]
        cos_cut = jnp.concatenate([cos_all[: self.seg]] * SEGS, axis=0)
        sin_cut = jnp.concatenate([sin_all[: self.seg]] * SEGS, axis=0)
        return jnp.where(self.single, cos_all, cos_cut), jnp.where(self.single, sin_all, sin_cut)

    def mod_row(self, block, part):
        row = self.slot * SEGS + jnp.where(self.single, 0, block)
        return self.mods[pl.ds(row, 1), part * self.width : (part + 1) * self.width]

    def add_segment(self, small, block, at, sums):
        row = 8 + jnp.where(self.single, 0, block)
        small[pl.ds(row, 1), at * self.width : (at + 1) * self.width] += sums

    def thirds(self, index):
        return [lanes(index, 128, p * self.width) for p in range(3)]


def forward(
    k, xv, win, wout, wex, wre, normed, qkv, probs, mixed, middle, modded, slope, active, branch,
    result, bias,
):
    span, width, held = k.span, k.width, k.held
    held.begin(xv, win)
    held.need(xv)
    unit, _ = norm_parts(xv[...].astype(F32))
    normed[...] = (unit * k.gain[...].astype(F32)).astype(BF16)
    held.done(normed)
    across = lax.broadcasted_iota(jnp.int32, (span, span), 0) // k.seg
    down = lax.broadcasted_iota(jnp.int32, (span, span), 1) // k.seg
    bias[...] = jnp.where((across == down) | k.single, 0.0, -1e30)
    held.need(win)
    held.begin(wout, wex, wre)
    cos_part, sin_part = k.trig_pair()
    for tile, factor in ((0, 0.125), (1, 1.0)):
        for i in range(width // 256):
            at = lanes(i, 256, tile * width)
            joint = dot(normed[...], win[:, at])
            outs = []
            for piece in (joint[:, :128], joint[:, 128:]):
                turned = piece * cos_part + swap_halves(piece, k.low_half) * sin_part
                outs.append((turned * factor).astype(BF16))
            qkv[:, at] = jnp.concatenate(outs, axis=1)
    qkv[:, 2 * width :] = dot(normed[...], win[:, 2 * width :]).astype(BF16)
    held.done(qkv)

    def heads(i):
        at = k.thirds(i)
        query, key, value = (qkv[:, a] for a in at)
        outs = []
        for h in range(2):
            scores = dot(key * k.head_row[h], query, 1, 1) + bias[...]
            top = jnp.max(scores, axis=0, keepdims=True)
            raised = jnp.exp(scores - top)
            total = jnp.sum(raised, axis=0, keepdims=True)
            prob = raised * (1.0 / total)
            probs[2 * i + h] = prob
            outs.append(dot(prob.astype(BF16), value, 0, 0))
        mixed[:, at[0]] = jnp.where(k.low_head, outs[0], outs[1]).astype(BF16)

    steps_of(k.pairs, 3, heads)
    held.done(probs, mixed)
    held.need(wout)
    middle[...] = xv[...].astype(F32) + dot(mixed[...], wout[...])
    held.done(middle)
    for b, rows in k.blocks:
        unit, _ = norm_parts(middle[rows])
        modded[rows] = (unit * (1.0 + k.mod_row(b, 0)) + k.mod_row(b, 1)).astype(BF16)
    held.done(modded)
    held.need(wex, wre)
    branch[...] = jnp.broadcast_to(k.rbias[...].astype(F32), (span, width))

    def feed(j):
        at = lanes(j, k.step)
        pre = dot(modded[...], wex[:, at]) + k.ebias[:, at].astype(F32)
        area = 0.5 + 0.5 * lax.erf(pre * ROOT_HALF)
        out = (pre * area).astype(BF16)
        if k.sloped:
            slope[:, at] = area + pre * (jnp.exp(pre * pre * -0.5) * ROOT_TAU)
        active[:, at] = out
        branch[...] += dot(out, wre[at, :])

    repeat(k.tiles, feed)
    held.done(slope, active, branch)
    for b, rows in k.blocks:
        result[rows] = (middle[rows] + k.mod_row(b, 2) * branch[rows]).astype(BF16)
    held.done(result)


def output(k, dyv, bgrad):
    k.later()
    k.held.need(dyv)
    for b, rows in k.blocks:
        bgrad[rows] = (dyv[rows].astype(F32) * k.mod_row(b, 2)).astype(BF16)
    k.held.done(bgrad)


def mlp(k, wre, wex, bgrad, slope, middle, branch, dyv, pgrad, agrad, middle_grad, small_m, acc):
    width, held = k.width, k.held
    small_m[...] = jnp.zeros(small_m.shape, F32)
    acc[...] = jnp.zeros(acc.shape, F32)
    held.need(bgrad, wre, slope)
    held.begin(wex, middle, dyv, branch)
    k.later()
    held.need(wex)

    def feed(j):
        at = lanes(j, k.step)
        grad = dot(bgrad[...], wre[at, :], 1, 1)
        pre_grad = (slope[:, at] * grad).astype(BF16)
        pgrad[:, at] = pre_grad
        small_m[0:1, at] = jnp.sum(pre_grad.astype(F32), axis=0, keepdims=True)
        acc[...] += dot(pre_grad, wex[:, at], 1, 1)

    repeat(k.tiles, feed)
    held.done(pgrad)
    held.need(middle, dyv, branch)
    total = jnp.zeros((1, width), F32)
    for b, rows in k.blocks:
        cotan = dyv[rows].astype(F32)
        total += jnp.sum(bgrad[rows].astype(F32), axis=0, keepdims=True)
        grad = acc[rows]
        unit, factor = norm_parts(middle[rows])
        k.add_segment(small_m, b, 0, jnp.sum(grad * unit, axis=0, keepdims=True))
        k.add_segment(small_m, b, 1, jnp.sum(grad, axis=0, keepdims=True))
        k.add_segment(small_m, b, 2, jnp.sum(cotan * branch[rows], axis=0, keepdims=True))
        back = norm_back(grad * (1.0 + k.mod_row(b, 0)), unit, factor)
        full = cotan + back
        middle_grad[rows] = full
        agrad[rows] = full.astype(BF16)
    small_m[1:2, :width] = total
    held.done(agrad, middle_grad, small_m)


def attend(
    k, wout, win, agrad, probs, qkv, xv, middle_grad, jgrad, leave, small_a, mixed_grad, acc
):
    held = k.held
    held.need(agrad, wout)
    held.begin(probs, qkv)
    mixed_grad[...] = dot(agrad[...], wout[...], 1, 1).astype(BF16)
    held.need(probs, qkv)
    held.begin(win, xv, middle_grad)
    k.later()
    cos_part, sin_part = k.trig_pair()

    def heads(i):
        at = k.thirds(i)
        query, key, value = (qkv[:, a] for a in at)
        out_grad = mixed_grad[:, at[0]]
        parts = []
        for h in range(2):
            prob = probs[2 * i + h]
            pull = dot(value * k.head_row[h], out_grad, 1, 1)
            shared = jnp.sum(prob * pull, axis=0, keepdims=True)
            score_grad = (prob * (pull - shared)).astype(BF16)
            parts.append(
                (
                    dot(score_grad, key, 0, 0),
                    dot(score_grad, query),
                    dot(prob.astype(BF16), out_grad),
                )
            )
        for p in range(3):
            grad = jnp.where(k.low_head, parts[0][p], parts[1][p])
            if p < 2:
                grad = grad * cos_part - swap_halves(grad, k.low_half) * sin_part
                if p == 0:
                    grad = grad * 0.125
            jgrad[:, at[p]] = grad.astype(BF16)

    steps_of(k.pairs, 3, heads)
    held.done(jgrad)
    held.need(win, xv, middle_grad)
    acc[...] = dot(jgrad[...], win[...], 1, 1)
    small_a[...] = jnp.zeros(small_a.shape, F32)
    total = jnp.zeros((1, k.width), F32)
    for b, rows in k.blocks:
        grad = acc[rows]
        unit, factor = norm_parts(xv[rows].astype(F32))
        total += jnp.sum(grad * unit, axis=0, keepdims=True)
        back = norm_back(grad * k.gain[...].astype(F32), unit, factor)
        leave[rows] = (middle_grad[rows] + back).astype(BF16)
    small_a[0:1, :] = total
    held.done(leave, small_a)


def term_tile(k, left, right, row, col):
    at, to = lanes(row, TILE), lanes(col, k.width)
    return sum(dot(a[:, at], b[:, to], 0, 0) for a, b in zip(left, right))


def put_pairs(k, total, lines, send, keep, first, at):
    for g in range(total.shape[0] // (2 * lines)):
        even = total[2 * g * lines : (2 * g + 1) * lines]
        odd = total[(2 * g + 1) * lines : (2 * g + 2) * lines]
        send[first + g, at] = jnp.where(k.low, odd, even).astype(BF16)
        keep[first + g, at] = jnp.where(k.low, even, odd)


def term_reduce(k, active_x, bgrad_x, active, bgrad, send_r, keep_r):
    lines = k.hidden // k.count
    group = TILE // (2 * lines)
    for row in range(k.hidden // TILE):
        total = term_tile(k, (active_x, active), (bgrad_x, bgrad), row, 0)
        put_pairs(k, total, lines, send_r, keep_r, row * group, slice(None))
        if row % 2:
            k.held.done(send_r, keep_r, at=(((row - 1) * group, 2 * group),))


def square_terms(k, left, right, send, keep, parts):
    lines = k.width // k.count
    group = TILE // (2 * lines)
    for col, part in enumerate(parts):
        for row in range(k.width // TILE):
            total = term_tile(k, left, right, row, col)
            at = slice(part * lines, (part + 1) * lines)
            put_pairs(k, total, lines, send, keep, row * group, at)
        k.held.done(send, keep, at=((0, k.count // 2), (part * lines, lines)))


def term_expand(
    k, modded_x, pgrad_x, mixed_x, agrad_x, small_m_x, modded, pgrad, mixed, agrad, small_m,
    send_e, keep_e, lines_v,
):
    width = k.width
    tall = k.hidden // width
    lines = width // k.count
    square_terms(k, (modded_x, modded), (pgrad_x, pgrad), send_e, keep_e, range(tall))
    square_terms(k, (mixed_x, mixed), (agrad_x, agrad), send_e, keep_e, (tall,))
    seqs = [item[8 : 8 + SEGS, : 3 * width] for item in (small_m_x, small_m)]
    times = sum(
        k.embed[:, n * SEGS + s : n * SEGS + s + 1] * seqs[n][s : s + 1]
        for n in range(2)
        for s in range(SEGS)
    )
    lines_v[0:1] = small_m_x[1:2, :width] + small_m[1:2, :width]
    bias_sum = jnp.sum(seqs[0] + seqs[1], axis=0, keepdims=True)
    for n in range(3):
        lines_v[1 + n : 2 + n] = bias_sum[:, n * width : (n + 1) * width]
    hidden_sum = small_m_x[0:1] + small_m[0:1]
    for n in range(tall):
        lines_v[4 + n : 5 + n] = hidden_sum[:, n * width : (n + 1) * width]
    deep = EMB // k.count
    first = (tall + 1) * lines
    size = 3 * deep + SMALL_ROWS
    for g in range(k.count // 2):
        even, odd = (
            jnp.concatenate(
                [
                    times[(2 * g + n) * deep : (2 * g + n + 1) * deep, p * width : (p + 1) * width]
                    for p in range(3)
                ]
                + [lines_v[...]],
                axis=0,
            )
            for n in range(2)
        )
        send_e[g, first : first + size] = jnp.where(k.low, odd, even).astype(BF16)
        keep_e[g, first : first + size] = jnp.where(k.low, even, odd)
    k.held.done(send_e, keep_e, at=((0, k.count // 2), (first, size)))


def term_attend(k, normed_x, jgrad_x, small_a_x, normed, jgrad, small_a, send_a, keep_a):
    lines = k.width // k.count
    square_terms(k, (normed_x, normed), (jgrad_x, jgrad), send_a, keep_a, range(3))
    total = small_a_x[0:1] + small_a[0:1]
    block = jnp.concatenate([total, jnp.zeros((GAIN_ROWS - 1, k.width), F32)], axis=0)
    at = slice(3 * lines, 3 * lines + GAIN_ROWS)
    for g in range(k.count // 2):
        send_a[g, at] = block.astype(BF16)
        keep_a[g, at] = block
    k.held.done(send_a, keep_a, at=((0, k.count // 2), (3 * lines, GAIN_ROWS)))


def plain_pieces(ops, count):
    def blocks(left, right):
        total = sum(dot(a, b, 0, 0) for a, b in zip(left, right))
        width = ops.bgrad[0].shape[1]
        parts = [total[:, i : i + width] for i in range(0, total.shape[1], width)]
        return [part.reshape(count, -1, width) for part in parts]

    reduce = blocks(ops.active, ops.bgrad)
    expand = blocks(ops.modded, ops.pgrad)
    last = blocks(ops.normed, ops.jgrad)
    expand += blocks(ops.mixed, ops.agrad)
    width = ops.bgrad[0].shape[1]
    seqs = jnp.concatenate([item[8 : 8 + SEGS, : 3 * width] for item in ops.small_m])
    times = jnp.dot(ops.embed, seqs, precision=lax.Precision.HIGHEST)
    expand += [times[:, i * width : (i + 1) * width].reshape(count, -1, width) for i in range(3)]
    lines = jnp.concatenate(
        [
            sum(item[1:2, :width] for item in ops.small_m),
            jnp.sum(seqs, axis=0).reshape(-1, width),
            sum(item[0] for item in ops.small_m).reshape(-1, width),
        ]
    )
    gain = jnp.pad(sum(item[0:1] for item in ops.small_a), ((0, GAIN_ROWS - 1), (0, 0)))
    expand.append(jnp.broadcast_to(lines, (count,) + lines.shape))
    last.append(jnp.broadcast_to(gain, (count,) + gain.shape))
    return [jnp.concatenate(item, axis=1) for item in (reduce, expand, last)]


def shapes_of(span, width, hidden, count):
    tok = lambda cols, kind=BF16: ((span, cols), kind)
    shapes = dict(
        xv=tok(width),
        dyv=tok(width),
        win=((width, 3 * width), BF16),
        wout=((width, width), BF16),
        wex=((width, hidden), BF16),
        wre=((hidden, width), BF16),
        normed=tok(width),
        qkv=tok(3 * width),
        probs=((HEADS, span, span), F32),
        mixed=tok(width),
        middle=tok(width, F32),
        modded=tok(width),
        slope=tok(hidden, F32),
        active=tok(hidden),
        branch=tok(width, F32),
        result=tok(width),
        bgrad=tok(width),
        pgrad=tok(hidden),
        agrad=tok(width),
        jgrad=tok(3 * width),
        mixed_grad=tok(width),
        middle_grad=tok(width, F32),
        leave=tok(width),
        acc=tok(width, F32),
        bias=tok(span, F32),
        small_m=((16, hidden), F32),
        small_a=((8, width), F32),
        lines_v=((SMALL_ROWS, width), F32),
    )
    shapes.update({item + "_x": shape for item, shape in shapes.items()})
    rows = dict(
        r=hidden // count,
        e=(hidden + width + 3 * EMB) // count + SMALL_ROWS,
        a=3 * width // count + GAIN_ROWS,
    )
    for item, lines in rows.items():
        shapes["send_" + item] = ((count // 2, lines, width), BF16)
        shapes["keep_" + item] = ((count // 2, lines, width), F32)
    return shapes


def uses(part):
    return list(inspect.signature(part).parameters)[1:]


def stage_kernel(sizes, parts, term, who, slot, plan, *refs):
    refs = list(refs)
    layer = Layer(sizes, slot, refs[:9])
    span = layer.span
    pos = 9
    cut = lambda ref, row: ref if row is None else ref.at[pl.ds(row, span)]
    sources = {}
    for name, row in plan.sources:
        sources[name] = cut(refs[pos], row)
        pos += 1
    pos += plan.extra
    stores = {}
    for name, row in plan.targets:
        stores[name] = cut(refs[pos], row)
        pos += 1
    bufs = {name: sources.pop(name) for name in plan.direct}
    for name in plan.bufs:
        bufs[name] = refs[pos]
        pos += 1
    mine_sems, both_sems, other_sems = refs[pos:]
    mine = layer.section == who
    loads = {name: ref for name, ref in sources.items() if name not in plan.shared}
    held = Held(bufs, loads, stores, mine_sems)
    common = Held(bufs, {name: sources[name] for name in plan.shared}, stores, both_sems)

    layer.sloped = "slope" in stores or mlp in parts
    layer.later = common.begin_all

    @pl.when(mine)
    def _():
        layer.held = held
        for part in parts:
            part(layer, *[bufs[name] for name in uses(part)])

    if term is not None:
        made = [name for name in uses(term) if name in plan.made]
        there = {name: stores.get(name, sources.get(name)) for name in made}
        other = Held(bufs, there, {}, other_sems)

        @pl.when(jnp.logical_not(mine))
        def _():
            common.waiting = set(common.loads)
            common.begin_all()
            other.need(*[bufs[name] for name in made])

        common.need(*[bufs[name] for name in plan.shared])
        layer.held = common
        term(layer, *[bufs[name] for name in uses(term)])
        common.finish()

    @pl.when(mine)
    def _():
        held.finish()


def stage(
    name, common, parts, who, slot, loads, stores, carried=None, after=(), term=None, firsts=None,
    shared=None,
):
    carried = carried or {}
    shared = dict(shared or {})
    span, width, hidden, count = common.sizes
    shapes = shapes_of(span, width, hidden, count)
    stores = dict(stores)
    if term is not None:
        for item in uses(term):
            if item.endswith("_x"):
                shared[item] = firsts[item[:-2]]
            if item.startswith(("send_", "keep_")):
                stores[item] = item
    loads = dict(loads, **shared)
    bufs = []
    for part in parts + ((term,) if term is not None else ()):
        bufs += [item for item in uses(part) if item not in bufs]
    direct = [item for item in bufs if isinstance(loads.get(item), list)]
    pair = lambda item: item if isinstance(item, tuple) else (item, None)
    args = list(common.args)
    in_specs = [pl.BlockSpec(memory_space=SMEM)] * 3 + [pl.BlockSpec(memory_space=VMEM)] * 6
    plan = Bag(sources=[], targets=[], direct=direct, shared=[], made=[])
    order = [item for item in loads if item in bufs]
    for item in order:
        if item in direct:
            array, row = loads[item][0], None
        else:
            array, row = pair(loads[item])
        args.append(array)
        in_specs.append(pl.BlockSpec(memory_space=VMEM if item in direct else ANY))
        plan.sources.append((item, row))
        if item in shared:
            plan.shared.append(item)
    outs, aliases, extra = [], {}, []
    targets = [(item, *pair(key)) for item, key in stores.items()]
    for i, (item, key, row) in enumerate(targets):
        shape, kind = shapes[item]
        if row is not None:
            shape = (common.tokens,) + shape[1:]
        outs.append(jax.ShapeDtypeStruct(shape, kind))
        plan.targets.append((item, row))
        if key in carried:
            aliases[len(args) + len(extra)] = i
            extra.append(carried[key])
    extra += list(after)
    args += extra
    in_specs += [pl.BlockSpec(memory_space=ANY)] * len(extra)
    plan.update(
        extra=len(extra),
        bufs=[item for item in bufs if item not in direct],
        made=[item for part in parts for item in uses(part)],
    )
    plan["made"] = [item for item in plan.made if item not in shared and item not in direct]
    results = pl.pallas_call(
        partial(stage_kernel, common.sizes, parts, term, who, slot, plan),
        out_shape=outs,
        in_specs=in_specs,
        out_specs=[pl.BlockSpec(memory_space=ANY)] * len(outs),
        input_output_aliases=aliases,
        scratch_shapes=[pltpu.VMEM(*shapes[item]) for item in plan.bufs]
        + [pltpu.SemaphoreType.DMA((n,)) for n in (32, 48, 8)],
        compiler_params=pltpu.CompilerParams(vmem_limit_bytes=56 * 1024 * 1024),
        name=name,
    )(*args)
    return Bag({key: value for (_, key, _), value in zip(targets, results)})


def bits_of(count):
    bits = count.bit_length() - 1
    assert 1 << bits == count
    return bits


class Chunk:
    def __init__(self, axis, terms, rows):
        self.axis = axis
        self.start, self.size = rows
        self.bits = list(range(bits_of(2 * terms[0].shape[0]) - 1, 0, -1))
        self.settled = []
        self.terms = []
        for term in terms:
            self.add(term, self.start)

    def add(self, term, start=0):
        left = [bit for bit in self.bits if bit not in self.settled]
        self.terms.append((term.reshape((2,) * len(left) + term.shape[-2:]), left, start))

    def take(self, term, start, left, flip):
        me = lax.axis_index(self.axis)
        side = lambda bit: 1 - ((me >> bit) & 1) if bit == flip else (me >> bit) & 1
        starts = [side(bit) if bit in self.settled else 0 for bit in left]
        sizes = [1 if bit in self.settled else 2 for bit in left]
        cols = term.shape[-1]
        piece = lax.dynamic_slice(term, starts + [start, 0], sizes + [self.size, cols])
        open_bits = [2] * (len(self.bits) - len(self.settled))
        return piece.reshape(open_bits + [self.size, cols]).astype(F32)

    def split(self, bit):
        self.settled.append(bit)
        return sum(self.take(term, start, left, bit) for term, left, start in self.terms).astype(
            BF16
        )

    def total(self):
        return sum(self.take(term, start, left, None) for term, left, start in self.terms)


def exchange(block, axis, bit):
    count = lax.axis_size(axis)
    return lax.ppermute(block, axis, [(i, i ^ (1 << bit)) for i in range(count)])


def join(*items):
    return lax.optimization_barrier(items)


def angle_table(span):
    half = HEAD // 2
    freqs = np.exp(-math.log(10000.0) * np.arange(half, dtype=np.float32) / half)
    phase = np.arange(span, dtype=np.float32)[:, None] * freqs.astype(np.float32)[None, :]
    cos_part, sin_part = np.cos(phase), np.sin(phase)
    return np.stack(
        [
            np.concatenate([cos_part] * 4, axis=1),
            np.concatenate([-sin_part, sin_part] * 2, axis=1),
        ]
    ).astype(np.float32)


def per_device(
    ends_in,
    lengths,
    times,
    norm_gain,
    attend_in,
    attend_out,
    time_weight,
    time_bias,
    expand_weight,
    expand_bias,
    reduce_weight,
    reduce_bias,
):
    local = ends_in[0]
    micro = lengths.shape[1]
    assert micro == 2
    width = local.shape[1]
    span = local.shape[0] // micro
    hidden = expand_weight.shape[2]
    count = lax.axis_size("rep")
    section = lax.axis_index("section")
    rank = lax.axis_index("rep")
    core = rank & 1
    steps = jnp.exp(-math.log(10000.0) * jnp.arange(EMB // 2, dtype=F32) / (EMB // 2))
    turn = times.reshape(micro * SEGS, 1).astype(F32) * steps
    embed = jnp.concatenate([jnp.cos(turn), jnp.sin(turn)], axis=1)
    mods = jnp.dot(
        embed, time_weight[0].astype(F32), precision=lax.Precision.HIGHEST
    ) + time_bias.astype(F32)
    common = Bag(
        args=(
            lengths[0],
            section.reshape(1),
            core.reshape(1),
            mods,
            jnp.asarray(angle_table(span)),
            embed.T,
            norm_gain,
            expand_bias,
            reduce_bias,
        ),
        sizes=(span, width, hidden, count),
        tokens=local.shape[0],
    )
    weights = Bag(
        win=attend_in[0], wout=attend_out[0], wex=expand_weight[0], wre=reduce_weight[0]
    )
    rows = [(local, slot * span) for slot in range(micro)]
    same = lambda *names: {name: name for name in names}
    whole = {
        name: name
        for part in (term_reduce, term_expand, term_attend)
        for name in uses(part)
        if name + "_x" in uses(part)
    }
    run = partial(stage, common=common)
    both = (forward, output, mlp, attend)
    over = lambda block, route: lax.ppermute(block, "section", route)
    a = run(
        "first_0",
        parts=(forward,),
        who=0,
        slot=0,
        loads=dict(xv=rows[0], **weights),
        stores=dict(result="leave"),
    )
    came_0 = over(a.leave, [(0, 1)])
    held = [item for item in uses(forward) if item not in weights]
    b = run(
        "first_1",
        parts=(forward,),
        who=0,
        slot=1,
        loads=dict(xv=rows[1], **weights),
        stores={item: item for item in held if item not in ("xv", "bias")},
        after=(a.leave,),
    )
    came_1 = over(b.result, [(0, 1)])
    x = run(
        "second_0",
        parts=both,
        who=1,
        slot=0,
        loads=dict(xv=[came_0], dyv=rows[0], **weights),
        stores=dict(whole, result=("ends", 0), leave="leave"),
        after=(b.result,),
    )
    back_0 = over(x.leave, [(1, 0)])
    y = run(
        "second_1",
        parts=both,
        who=1,
        slot=1,
        loads=dict(xv=[came_1], dyv=rows[1], **weights),
        stores=dict(whole, result=("ends", span), leave="leave"),
        carried=dict(b, ends=x.ends),
        after=(x.leave,),
    )
    back_1 = over(y.leave, [(1, 0)])
    x = run(
        "back_0",
        parts=both,
        who=0,
        slot=0,
        loads=dict(xv=rows[0], dyv=[back_0], **weights),
        stores=dict(whole, leave=("ends", 0)),
        carried=dict(x, ends=y.ends),
        after=(y.leave,),
    )
    fused = width // count % 16 == 0 and TILE % (2 * hidden // count) == 0

    def last(name, part, loads, stores, term, shared, after=()):
        y.update(
            run(
                name,
                parts=(part,),
                who=0,
                slot=1,
                loads=loads,
                stores=stores,
                carried=dict(y, ends=x.ends),
                after=after,
                term=term if fused else None,
                firsts=x,
                shared=shared if fused else None,
            )
        )

    last("back_1_out", output, dict(dyv=[back_1]), same("bgrad"), term_reduce, dict(active=y.active))
    last_mlp = partial(
        last,
        "back_1_mlp",
        mlp,
        dict(
            wre=weights.wre,
            bgrad=y.bgrad,
            slope=b.slope,
            wex=weights.wex,
            middle=b.middle,
            branch=b.branch,
            dyv=[back_1],
        ),
        same("pgrad", "agrad", "middle_grad", "small_m"),
        term_expand,
        dict(modded=y.modded, mixed=y.mixed),
    )

    def last_attend(after):
        last(
            "back_1_attend",
            attend,
            dict(
                wout=weights.wout,
                agrad=y.agrad,
                probs=b.probs,
                qkv=b.qkv,
                win=weights.win,
                xv=rows[1],
                middle_grad=y.middle_grad,
            ),
            dict(same("jgrad", "small_a"), leave=("ends", span)),
            term_attend,
            dict(normed=y.normed),
            after=after,
        )

    if not fused:
        last_mlp()
        last_attend(())
        ops = Bag({item: (x[item], y[item]) for item in whole}, embed=embed.T)
        for item, total in zip("rea", plain_pieces(ops, count)):
            view = total.reshape((count // 2, 2) + total.shape[1:])
            side = lambda at: lax.dynamic_index_in_dim(view, at, 1, keepdims=False)
            y["send_" + item] = side(1 - core).astype(BF16)
            y["keep_" + item] = side(core)
    swap = lambda block, bit: exchange(block, "rep", bit)
    bits = bits_of(count)

    def halves(came, keep, share):
        lines = keep.shape[1]
        cut = lines * share // 100 // 16 * 16
        terms = [keep, came]
        return Chunk("rep", terms, (0, cut)), Chunk("rep", terms, (cut, lines - cut))

    r1, r2 = halves(swap(y.send_r, 0), y.keep_r, 50)
    send_1, send_2 = r1.split(1), r2.split(2)
    came_r1, came_r2 = swap(send_1, 1), swap(send_2, 2)
    if fused:
        last_mlp(after=(send_1, send_2))
    came_r1, came_r2, send_e = join(came_r1, came_r2, y.send_e)
    came_e = swap(send_e, 0)
    r1.add(came_r1)
    r2.add(came_r2)
    send_1, send_2 = r1.split(2), r2.split(1)
    came_r1, came_r2 = swap(send_1, 2), swap(send_2, 1)
    came_e, _, _ = join(came_e, send_1, send_2)
    e1, e2 = halves(came_e, y.keep_e, 50)
    send_1, send_2 = e1.split(1), e2.split(2)
    came_e1, came_e2 = swap(send_1, 1), swap(send_2, 2)
    if fused:
        last_attend((send_1, send_2))
    ends = y.ends
    came_r1, came_r2, came_e1, came_e2, send_a = join(
        came_r1, came_r2, came_e1, came_e2, y.send_a
    )
    came_a = swap(send_a, 0)
    e1.add(came_e1)
    e2.add(came_e2)
    send_1, send_2 = e1.split(2), e2.split(1)
    came_e1, came_e2 = swap(send_1, 2), swap(send_2, 1)
    came_r1, came_r2, _, _ = join(came_r1, came_r2, send_1, send_2)
    r1.add(came_r1)
    r2.add(came_r2)
    block_r = jnp.concatenate([r1.split(3), r2.split(3)], axis=-2)
    came_r = swap(block_r, 3)
    came_a, came_e1, came_e2, _ = join(came_a, came_e1, came_e2, block_r)
    a1, a2 = halves(came_a, y.keep_a, 60)
    send_1, send_2 = a1.split(1), a2.split(2)
    came_a1, came_a2 = swap(send_1, 1), swap(send_2, 2)
    came_e1, came_e2, _, _ = join(came_e1, came_e2, send_1, send_2)
    e1.add(came_e1)
    e2.add(came_e2)
    block_e = jnp.concatenate([e1.split(3), e2.split(3)], axis=-2)
    came_e = swap(block_e, 3)
    came_r, _ = join(came_r, block_e)
    r1.add(came_r[..., : r1.size, :])
    r2.add(came_r[..., r1.size :, :])
    came_a1, came_a2, _ = join(came_a1, came_a2, came_r)
    a1.add(came_a1)
    a2.add(came_a2)
    send_1, send_2 = a1.split(2), a2.split(1)
    came_a1, came_a2 = swap(send_1, 2), swap(send_2, 1)
    a1.add(came_a1)
    a2.add(came_a2)
    block_a = jnp.concatenate([a1.split(3), a2.split(3)], axis=-2)
    came_a = swap(block_a, 3)
    came_e, _ = join(came_e, block_a)
    e1.add(came_e[..., : e1.size, :])
    e2.add(came_e[..., e1.size :, :])
    a1.add(came_a[..., : a1.size, :])
    a2.add(came_a[..., a1.size :, :])
    for bit in range(4, bits):
        for chunk in (r1, r2, e1, e2, a1, a2):
            chunk.add(swap(chunk.split(bit), bit))
    share_r, share_e, share_a = (
        jnp.concatenate([one.total(), two.total()]) for one, two in ((r1, r2), (e1, e2), (a1, a2))
    )
    lines = width // count
    deep = EMB // count
    tall = hidden // width
    side = lambda item, n, size: jnp.concatenate(
        [item[i * size : (i + 1) * size] for i in range(n)], axis=1
    )
    at_o = tall * lines
    at_t = at_o + lines
    small = share_e[at_t + 3 * deep :]
    flat = lambda item, first, n: lax.dynamic_slice_in_dim(
        item[first : first + n].reshape(-1), rank * (n * width // count), n * width // count
    )
    results = (
        flat(share_a, 3 * lines, 1),
        side(share_a, 3, lines),
        share_e[at_o:at_t],
        side(share_e[at_t:], 3, deep),
        flat(small, 1, 3),
        side(share_e, tall, lines),
        flat(small, 4, tall),
        share_r,
        flat(small, 0, 1),
    )
    return (ends[None],) + tuple(piece[None] for piece in results)


def solution(mesh):
    return jax.shard_map(
        per_device,
        mesh=mesh,
        in_specs=(
            P("section", "rep", None),
            P("rep", None, None),
            P("rep", None, None),
            P("section", None),
            P("section", None, None),
            P("section", None, None),
            P("section", None, None),
            P("section", None),
            P("section", None, None),
            P("section", None),
            P("section", None, None),
            P("section", None),
        ),
        out_specs=(
            P("section", "rep", None),
            P("section", "rep"),
            P("section", "rep", None),
            P("section", "rep", None),
            P("section", "rep", None),
            P("section", "rep"),
            P("section", "rep", None),
            P("section", "rep"),
            P("section", "rep", None),
            P("section", "rep"),
        ),
        check_vma=False,
    )
```

profile of v0, /device:TPU:0, one launch (start us, length us, event | category | flops | bytes accessed | tf_op | source)
XLA Modules:
  0.0 250.1 jit_solution(8769967038510919890)
XLA Ops:
  4.1 12.0 %first_0.1.refs_14_ = bf16[256,768]{1,0:T(8,128)(2,1)} custom-call(s32[2,4]{1,0:T(2,128)} %bitcast.337, s32[1]{0:T(128)} %bitcast.1.refs_1_, s32[1]{0:T(128)} %bitcast.2.refs_2_, f32[8,2304]{1,0:T(8,128)} %convolution_add_fusion.refs_3_, f32[2,256,128]{2,1,0:T(8,128)} %constant.45.clone.refs_4_, f32[128,8]{1,0:T(8,128)} %bitcast.311, ...), custom_call_target="tpu_custom_call" | custom-call | tf_op jit(solution)/shard_map/first_0/pallas_call | solution.py:618
  16.2 1.3 collective-permute-start.1
  17.5 14.2 %first_1.1 = (bf16[256,768]{1,0:T(8,128)(2,1)}, bf16[256,2304]{1,0:T(8,128)(2,1)}, f32[12,256,256]{2,1,0:T(8,128)}, bf16[256,768]{1,0:T(8,128)(2,1)}, f32[256,76...) custom-call(s32[2,4]{1,0:T(2,128)} %bitcast.338, ...), custom_call_target="tpu_custom_call" | custom-call | tf_op jit(solution)/shard_map/first_1/pallas_call | solution.py:618
  31.7 1.3 collective-permute-start
  33.8 11.0 %second_0.1 = (bf16[256,3072]{1,0:T(8,128)(2,1)}, bf16[256,768]{1,0:T(8,128)(2,1)}, bf16[256,768]{1,0:T(8,128)(2,1)}, bf16[256,3072]{1,0:T(8,128)(2,1)}, bf16[25...) custom-call(s32[2,4]{1,0:T(2,128)} %bitcast.339, ...), custom_call_target="tpu_custom_call" | custom-call | tf_op jit(solution)/shard_map/second_0/pallas_call | solution.py:618
  44.9 1.3 collective-permute-start.3
  46.9 6.6 %second_1.1 = (bf16[256,3072]{1,0:T(8,128)(2,1)}, bf16[256,768]{1,0:T(8,128)(2,1)}, bf16[256,768]{1,0:T(8,128)(2,1)}, bf16[256,3072]{1,0:T(8,128)(2,1)}, bf16[25...) custom-call(s32[2,4]{1,0:T(2,128)} %bitcast.340, ...), custom_call_target="tpu_custom_call", output_to_operand_aliasing={{0}: (15, {}), {2}: (16, {}), {4}: (17, {}), {7}: (18, {}),... | custom-call | tf_op jit(solution)/shard_map/second_1/pallas_call | solution.py:618
  53.5 1.3 collective-permute-start.2
  54.8 18.0 %collective-permute-done.3.refs_10_ = bf16[256,768]{1,0:T(8,128)(2,1)S(1)} collective-permute-done((bf16[256,768]{1,0:T(8,128)(2,1)}, bf16[256,768]{1,0:T(8,128)(2,1)S(1)}, u32[]{:S(2)}, u32[]{:S(2)}) %collective-permute-start.3) | collective-permute-done | bytes 393248 | tf_op jit(solution)/shard_map/ppermute | solution.py:752
  73.6 21.7 %back_0.1 = (bf16[256,3072]{1,0:T(8,128)(2,1)}, bf16[256,768]{1,0:T(8,128)(2,1)}, bf16[256,768]{1,0:T(8,128)(2,1)}, bf16[256,3072]{1,0:T(8,128)(2,1)}, bf16[256,...) custom-call(s32[2,4]{1,0:T(2,128)} %bitcast.341, ...), custom_call_target="tpu_custom_call", output_to_operand_aliasing={{0}: (15, {}), {1}: (16, {}), {2}: (17, {}), {3}: (18, {}),... | custom-call | tf_op jit(solution)/shard_map/back_0/pallas_call | solution.py:618
  95.3 3.0 %collective-permute-done.2.refs_9_.refs_15_ = bf16[256,768]{1,0:T(8,128)(2,1)S(1)} collective-permute-done((bf16[256,768]{1,0:T(8,128)(2,1)}, bf16[256,768]{1,0:T(8,128)(2,1)S(1)}, u32[]{:S(2)}, u32[]{:S(2)}) %collective-permute-start.2) | collective-permute-done | bytes 393248 | tf_op jit(solution)/shard_map/ppermute | solution.py:752
  99.1 8.0 %back_1_out.1 = (bf16[256,768]{1,0:T(8,128)(2,1)}, bf16[8,192,768]{2,1,0:T(8,128)(2,1)}, f32[8,192,768]{2,1,0:T(8,128)}) custom-call(s32[2,4]{1,0:T(2,128)} %bitcast.342, s32[1]{0:T(128)} %bitcast.1.refs_1_, s32[1]{0:T(128)} %bitcast.2.refs_2_, f32[8,2304]{1,0:T(8,128)} %convolution_add_fusion.refs_3_, ...), custom_call_target="tpu_custom_call", output_to_operand_aliasing={{0}: (13, {})} | custom-call | tf_op jit(solution)/shard_map/back_1_out/pallas_call | solution.py:618
  107.1 4.7 %collective-permute-done.4 = bf16[8,192,768]{2,1,0:T(8,128)(2,1)S(1)} collective-permute-done((bf16[8,192,768]{2,1,0:T(8,128)(2,1)}, bf16[8,192,768]{2,1,0:T(8,128)(2,1)S(1)}, u32[]{:S(2)}, u32[]{:S(2)}) %collective-permute-start.4) | collective-permute-done | bytes 2359328 | tf_op jit(solution)/shard_map/ppermute | solution.py:674
  111.9 1.4 fusion.14.refs_27_
  113.3 1.6 fusion.13.refs_26_
  114.9 1.9 collective-permute-start.6
  116.8 1.5 collective-permute-start.5
  118.3 18.2 %back_1_mlp.1 = (bf16[256,3072]{1,0:T(8,128)(2,1)}, bf16[256,768]{1,0:T(8,128)(2,1)}, f32[256,768]{1,0:T(8,128)}, f32[16,3072]{1,0:T(8,128)}, bf16[8,272,768]{2,1,0:T(8,128)(2,1)}, /*index=5*/f32[8,272,768]{2,1,0:T(8,128)}) custom-call(s32[2,4]{1,0:T(2,128)} %bitcast.343, ...), custom_call_target="tpu_custom_call", output_to_operand_aliasing={{0}: (23, {}), {1}: (24, {}), {3}: (25, {})} | custom-call | tf_op jit(solution)/shard_map/back_1_mlp/pallas_call | solution.py:618
  136.6 1.7 fusion.23
  138.3 4.5 %collective-permute-done.7 = bf16[8,272,768]{2,1,0:T(8,128)(2,1)} collective-permute-done((bf16[8,272,768]{2,1,0:T(8,128)(2,1)}, bf16[8,272,768]{2,1,0:T(8,128)(2,1)}, u32[]{:S(2)}, u32[]{:S(2)}) %collective-permute-start.7) | collective-permute-done | bytes 3342368 | tf_op jit(solution)/shard_map/ppermute | solution.py:674
  142.9 1.9 fusion.4.refs_24_
  145.3 1.8 fusion.8.refs_23_
  147.4 1.8 collective-permute-start.8
  149.2 1.5 collective-permute-start.9
  150.7 14.8 %back_1_attend.1 = (bf16[256,2304]{1,0:T(8,128)(2,1)}, f32[8,768]{1,0:T(8,128)}, bf16[512,768]{1,0:T(8,128)(2,1)}, bf16[8,160,768]{2,1,0:T(8,128)(2,1)}, f32[8,160,768]{2,1,0:T(8,128)}) custom-call(s32[2,4]{1,0:T(2,128)} %bitcast.344, s32[1]{0:T(128)} %bitcast.1.refs_1_, ...), custom_call_target="tpu_custom_call", output_to_operand_aliasing={{0}: (20, {}), {1}: (21, {}), {2}: (22, {})} | custom-call | tf_op jit(solution)/shard_map/back_1_attend/pallas_call | solution.py:618
  165.5 7.3 %collective-permute-done.8 = bf16[2,96,768]{2,1,0:T(8,128)(2,1)S(1)} collective-permute-done((bf16[2,96,768]{2,1,0:T(8,128)(2,1)S(1)}, bf16[2,96,768]{2,1,0:T(8,128)(2,1)S(1)}, u32[]{:S(2)}, u32[]{:S(2)}) %collective-permute-start.8) | collective-permute-done | bytes 294944 | tf_op jit(solution)/shard_map/ppermute | solution.py:674
  172.9 2.5 %fusion.7 = bf16[2,144,768]{2,1,0:T(8,128)(2,1)} fusion(f32[2,2,2,272,768]{4,3,2,1,0:T(8,128)} %bitcast.305, s32[]{:T(128)S(6)} %select_n.21, s32[]{:T(128)S(6)} %select_n.18, bf16[2,2,2,272,768]{4,3,2,1,0:T(8,128)(2,1)} %bitcast.19, bf16[2,2,144,768]{3,2,1,0:T(8,128)(2,1)S(1)} %collective-permute-done.11), kind=kLoop, calls=%fused_computation.14 | loop fusion | flops 1105920 | bytes 2211848 | tf_op jit(solution)/shard_map/convert_element_type | solution.py:664
  175.9 2.1 fusion.11
  178.0 1.5 collective-permute-start.13
  179.5 1.3 fusion.39
  181.6 7.7 %collective-permute-done.13 = bf16[2,128,768]{2,1,0:T(8,128)(2,1)} collective-permute-done((bf16[2,128,768]{2,1,0:T(8,128)(2,1)}, bf16[2,128,768]{2,1,0:T(8,128)(2,1)}, u32[]{:S(2)}, u32[]{:S(2)}) %collective-permute-start.13) | collective-permute-done | bytes 393248 | tf_op jit(solution)/shard_map/ppermute | solution.py:674
  189.3 2.4 fusion.12
  191.6 1.6 collective-permute-start.15
  193.2 2.0 fusion.30
  195.2 1.5 collective-permute-start.16
  196.7 2.6 %collective-permute-start.17 = (bf16[192,768]{1,0:T(8,128)(2,1)}, bf16[192,768]{1,0:T(8,128)(2,1)S(1)}, u32[]{:S(2)}, u32[]{:S(2)}) collective-permute-start(bf16[192,768]{1,0:T(8,128)(2,1)} %pad_maximum_fusion.2), channel_id=1, source_target_pairs={{0,8},{1,9},{2,10},{3,11},{4,12},{5,13},{6,14},{7,15},{8,0},{9,1},... | collective-permute-start | bytes 884744 | tf_op jit(solution)/shard_map/ppermute | solution.py:674
  199.3 1.3 fusion.33
  200.6 1.3 fusion.29
  202.4 10.6 %collective-permute-done.17 = bf16[192,768]{1,0:T(8,128)(2,1)S(1)} collective-permute-done((bf16[192,768]{1,0:T(8,128)(2,1)}, bf16[192,768]{1,0:T(8,128)(2,1)S(1)}, u32[]{:S(2)}, u32[]{:S(2)}) %collective-permute-start.17) | collective-permute-done | bytes 294944 | tf_op jit(solution)/shard_map/ppermute | solution.py:674
  213.8 1.3 fusion.20
  215.1 8.2 %collective-permute-start.19 = (bf16[2,96,768]{2,1,0:T(8,128)(2,1)S(1)}, bf16[2,96,768]{2,1,0:T(8,128)(2,1)S(1)}, u32[]{:S(2)}, u32[]{:S(2)}) collective-permute-start(bf16[2,96,768]{2,1,0:T(8,128)(2,1)S(1)} %fusion.20), channel_id=1, source_target_pairs={{0,4},{1,5},{2,6},{3,7},{4,0},{5,1},{6,2},{7,3},{8,12},{9,13},{10,... | collective-permute-start | bytes 884744 | tf_op jit(solution)/shard_map/ppermute | solution.py:674
  225.1 1.3 fusion.35
  227.3 3.0 %collective-permute-done.18 = bf16[2,64,768]{2,1,0:T(8,128)(2,1)S(1)} collective-permute-done((bf16[2,64,768]{2,1,0:T(8,128)(2,1)S(1)}, bf16[2,64,768]{2,1,0:T(8,128)(2,1)S(1)}, u32[]{:S(2)}, u32[]{:S(2)}) %collective-permute-start.18) | collective-permute-done | bytes 196640 | tf_op jit(solution)/shard_map/ppermute | solution.py:674
  232.7 1.2 fusion.37
  233.9 1.3 fusion.31
  235.3 1.3 fusion.28
  236.7 2.7 %collective-permute-start.20 = (bf16[160,768]{1,0:T(8,128)(2,1)S(1)}, bf16[160,768]{1,0:T(8,128)(2,1)S(1)}, u32[]{:S(2)}, u32[]{:S(2)}) collective-permute-start(bf16[160,768]{1,0:T(8,128)(2,1)S(1)} %pad_maximum_fusion.3), channel_id=1, source_target_pairs={{0,8},{1,9},{2,10},{3,11},{4,12},{5,13},{6,14},{7,15},{8,0},{9,1},... | collective-permute-start | bytes 737288 | tf_op jit(solution)/shard_map/ppermute | solution.py:674
  243.4 2.7 %collective-permute-done.20 = bf16[160,768]{1,0:T(8,128)(2,1)S(1)} collective-permute-done((bf16[160,768]{1,0:T(8,128)(2,1)S(1)}, bf16[160,768]{1,0:T(8,128)(2,1)S(1)}, u32[]{:S(2)}, u32[]{:S(2)}) %collective-permute-start.20) | collective-permute-done | bytes 245792 | tf_op jit(solution)/shard_map/ppermute | solution.py:674
  (92 shorter events, 22.8 us)
Async XLA Ops:
  0.6 2.5 %copy-start = (bf16[1,128,2304]{2,1,0:T(8,128)(2,1)S(1)}, bf16[1,128,2304]{2,1,0:T(8,128)(2,1)}, u32[]{:S(2)}) copy-start(bf16[1,128,2304]{2,1,0:T(8,128)(2,1)} %param.19) | copy-start | bytes 1769476
  16.2 16.9 %collective-permute-start.1 = (bf16[256,768]{1,0:T(8,128)(2,1)}, bf16[256,768]{1,0:T(8,128)(2,1)S(1)}, u32[]{:S(2)}, u32[]{:S(2)}) collective-permute-start(bf16[256,768]{1,0:T(8,128)(2,1)} %first_0.1.refs_14_), channel_id=1, source_target_pairs={{0,16},{1,17},{2,18},{3,19},{4,20},{5,21},{6,22},{7,23},{8,24},{9,... | collective-permute-start | bytes 1179656 | tf_op jit(solution)/shard_map/ppermute | solution.py:752
  31.7 14.4 %collective-permute-start = (bf16[256,768]{1,0:T(8,128)(2,1)}, bf16[256,768]{1,0:T(8,128)(2,1)S(1)}, u32[]{:S(2)}, u32[]{:S(2)}) collective-permute-start(bf16[256,768]{1,0:T(8,128)(2,1)} %get-tuple-element.85.refs_15_), channel_id=1, source_target_pairs={{0,16},{1,17},{2,18},{3,19},{4,20},{5,21},{6,22},{7,23},{8,24},{9,... | collective-permute-start | bytes 1179656 | tf_op jit(solution)/shard_map/ppermute | solution.py:752
  33.1 0.7 copy-start.12
  44.9 28.0 %collective-permute-start.3 = (bf16[256,768]{1,0:T(8,128)(2,1)}, bf16[256,768]{1,0:T(8,128)(2,1)S(1)}, u32[]{:S(2)}, u32[]{:S(2)}) collective-permute-start(bf16[256,768]{1,0:T(8,128)(2,1)} %get-tuple-element.91.refs_20_), channel_id=1, source_target_pairs={{16,0},{17,1},{18,2},{19,3},{20,4},{21,5},{22,6},{23,7},{24,8},{25... | collective-permute-start | bytes 1179656 | tf_op jit(solution)/shard_map/ppermute | solution.py:752
  46.2 0.7 copy-start.11
  53.5 44.8 %collective-permute-start.2 = (bf16[256,768]{1,0:T(8,128)(2,1)}, bf16[256,768]{1,0:T(8,128)(2,1)S(1)}, u32[]{:S(2)}, u32[]{:S(2)}) collective-permute-start(bf16[256,768]{1,0:T(8,128)(2,1)} %get-tuple-element.92.refs_26_), channel_id=1, source_target_pairs={{16,0},{17,1},{18,2},{19,3},{20,4},{21,5},{22,6},{23,7},{24,8},{25... | collective-permute-start | bytes 1179656 | tf_op jit(solution)/shard_map/ppermute | solution.py:752
  72.8 0.7 copy-start.10
  98.3 0.7 copy-start.6
  107.1 4.8 %collective-permute-start.4 = (bf16[8,192,768]{2,1,0:T(8,128)(2,1)}, bf16[8,192,768]{2,1,0:T(8,128)(2,1)S(1)}, u32[]{:S(2)}, u32[]{:S(2)}) collective-permute-start(bf16[8,192,768]{2,1,0:T(8,128)(2,1)} %get-tuple-element.123), channel_id=1, source_target_pairs={{0,1},{1,0},{2,3},{3,2},{4,5},{5,4},{6,7},{7,6},{8,9},{9,8},{10,11... | collective-permute-start | bytes 7077896 | tf_op jit(solution)/shard_map/ppermute | solution.py:674
  113.3 5.0 %copy-start.5 = (bf16[2,2,96,768]{3,2,1,0:T(8,128)(2,1)}, bf16[2,2,96,768]{3,2,1,0:T(8,128)(2,1)S(1)}, u32[]{:S(2)}) copy-start(bf16[2,2,96,768]{3,2,1,0:T(8,128)(2,1)S(1)} %fusion.14.refs_27_) | copy-start | bytes 1769476
  114.9 3.4 %copy-start.4 = (bf16[2,2,96,768]{3,2,1,0:T(8,128)(2,1)}, bf16[2,2,96,768]{3,2,1,0:T(8,128)(2,1)S(1)}, u32[]{:S(2)}) copy-start(bf16[2,2,96,768]{3,2,1,0:T(8,128)(2,1)S(1)} %fusion.13.refs_26_) | copy-start | bytes 1769476
  114.9 21.6 %collective-permute-start.6 = (bf16[2,2,96,768]{3,2,1,0:T(8,128)(2,1)S(1)}, bf16[2,2,96,768]{3,2,1,0:T(8,128)(2,1)S(1)}, u32[]{:S(2)}, u32[]{:S(2)}) collective-permute-start(bf16[2,2,96,768]{3,2,1,0:T(8,128)(2,1)S(1)} %fusion.14.refs_27_), channel_id=1, source_target_pairs={{0,4},{1,5},{2,6},{3,7},{4,0},{5,1},{6,2},{7,3},{8,12},{9,13},{10,... | collective-permute-start | bytes 1769480 | tf_op jit(solution)/shard_map/ppermute | solution.py:674
  116.8 19.7 %collective-permute-start.5 = (bf16[2,2,96,768]{3,2,1,0:T(8,128)(2,1)S(1)}, bf16[2,2,96,768]{3,2,1,0:T(8,128)(2,1)S(1)}, u32[]{:S(2)}, u32[]{:S(2)}) collective-permute-start(bf16[2,2,96,768]{3,2,1,0:T(8,128)(2,1)S(1)} %fusion.13.refs_26_), channel_id=1, source_target_pairs={{0,2},{1,3},{2,0},{3,1},{4,6},{5,7},{6,4},{7,5},{8,10},{9,11},{10,... | collective-permute-start | bytes 1769480 | tf_op jit(solution)/shard_map/ppermute | solution.py:674
  136.5 6.4 %copy-start.8 = (bf16[2,2,96,768]{3,2,1,0:T(8,128)(2,1)}, bf16[2,2,96,768]{3,2,1,0:T(8,128)(2,1)S(1)}, u32[]{:S(2)}) copy-start(bf16[2,2,96,768]{3,2,1,0:T(8,128)(2,1)S(1)} %collective-permute-done.6) | copy-start | bytes 1769476
  136.5 6.4 %copy-start.9 = (bf16[2,2,96,768]{3,2,1,0:T(8,128)(2,1)}, bf16[2,2,96,768]{3,2,1,0:T(8,128)(2,1)S(1)}, u32[]{:S(2)}) copy-start(bf16[2,2,96,768]{3,2,1,0:T(8,128)(2,1)S(1)} %collective-permute-done.5) | copy-start | bytes 1769476
  136.5 6.3 %collective-permute-start.7 = (bf16[8,272,768]{2,1,0:T(8,128)(2,1)}, bf16[8,272,768]{2,1,0:T(8,128)(2,1)}, u32[]{:S(2)}, u32[]{:S(2)}) collective-permute-start(bf16[8,272,768]{2,1,0:T(8,128)(2,1)} %get-tuple-element.137), channel_id=1, source_target_pairs={{0,1},{1,0},{2,3},{3,2},{4,5},{5,4},{6,7},{7,6},{8,9},{9,8},{10,11... | collective-permute-start | bytes 10027016 | tf_op jit(solution)/shard_map/ppermute | solution.py:674
  144.8 6.0 %copy-start.2 = (bf16[2,2,144,768]{3,2,1,0:T(8,128)(2,1)}, bf16[2,2,144,768]{3,2,1,0:T(8,128)(2,1)S(1)}, u32[]{:S(2)}) copy-start(bf16[2,2,144,768]{3,2,1,0:T(8,128)(2,1)S(1)} %fusion.4.refs_24_) | copy-start | bytes 2654212
  144.8 28.1 %collective-permute-start.11 = (bf16[2,2,144,768]{3,2,1,0:T(8,128)(2,1)S(1)}, bf16[2,2,144,768]{3,2,1,0:T(8,128)(2,1)S(1)}, u32[]{:S(2)}, u32[]{:S(2)}) collective-permute-start(bf16[2,2,144,768]{3,2,1,0:T(8,128)(2,1)S(1)} %fusion.4.refs_24_), channel_id=1, source_target_pairs={{0,4},{1,5},{2,6},{3,7},{4,0},{5,1},{6,2},{7,3},{8,12},{9,13},{10,... | collective-permute-start | bytes 2654216 | tf_op jit(solution)/shard_map/ppermute | solution.py:674
  147.1 3.7 %copy-start.3 = (bf16[2,2,128,768]{3,2,1,0:T(8,128)(2,1)}, bf16[2,2,128,768]{3,2,1,0:T(8,128)(2,1)S(1)}, u32[]{:S(2)}) copy-start(bf16[2,2,128,768]{3,2,1,0:T(8,128)(2,1)S(1)} %fusion.8.refs_23_) | copy-start | bytes 2359300
  147.1 25.8 %collective-permute-start.10 = (bf16[2,2,128,768]{3,2,1,0:T(8,128)(2,1)S(1)}, bf16[2,2,128,768]{3,2,1,0:T(8,128)(2,1)S(1)}, u32[]{:S(2)}, u32[]{:S(2)}) collective-permute-start(bf16[2,2,128,768]{3,2,1,0:T(8,128)(2,1)S(1)} %fusion.8.refs_23_), channel_id=1, source_target_pairs={{0,2},{1,3},{2,0},{3,1},{4,6},{5,7},{6,4},{7,5},{8,10},{9,11},{10,... | collective-permute-start | bytes 2359304 | tf_op jit(solution)/shard_map/ppermute | solution.py:674
  147.4 25.4 %collective-permute-start.8 = (bf16[2,96,768]{2,1,0:T(8,128)(2,1)S(1)}, bf16[2,96,768]{2,1,0:T(8,128)(2,1)S(1)}, u32[]{:S(2)}, u32[]{:S(2)}) collective-permute-start(bf16[2,96,768]{2,1,0:T(8,128)(2,1)S(1)} %get-tuple-element.165), channel_id=1, source_target_pairs={{0,4},{1,5},{2,6},{3,7},{4,0},{5,1},{6,2},{7,3},{8,12},{9,13},{10,... | collective-permute-start | bytes 884744 | tf_op jit(solution)/shard_map/ppermute | solution.py:674
  149.2 23.6 %collective-permute-start.9 = (bf16[2,96,768]{2,1,0:T(8,128)(2,1)S(1)}, bf16[2,96,768]{2,1,0:T(8,128)(2,1)S(1)}, u32[]{:S(2)}, u32[]{:S(2)}) collective-permute-start(bf16[2,96,768]{2,1,0:T(8,128)(2,1)S(1)} %get-tuple-element.164), channel_id=1, source_target_pairs={{0,2},{1,3},{2,0},{3,1},{4,6},{5,7},{6,4},{7,5},{8,10},{9,11},{10,... | collective-permute-start | bytes 884744 | tf_op jit(solution)/shard_map/ppermute | solution.py:674
  172.8 5.2 %copy-start.13 = (bf16[2,96,768]{2,1,0:T(8,128)(2,1)}, bf16[2,96,768]{2,1,0:T(8,128)(2,1)S(1)}, u32[]{:S(2)}) copy-start(bf16[2,96,768]{2,1,0:T(8,128)(2,1)S(1)} %collective-permute-done.9) | copy-start | bytes 884740
  172.8 3.1 %copy-start.7 = (bf16[2,2,128,768]{3,2,1,0:T(8,128)(2,1)}, bf16[2,2,128,768]{3,2,1,0:T(8,128)(2,1)S(1)}, u32[]{:S(2)}) copy-start(bf16[2,2,128,768]{3,2,1,0:T(8,128)(2,1)S(1)} %collective-permute-done.10) | copy-start | bytes 2359300
  172.9 16.4 %collective-permute-start.12 = (bf16[8,160,768]{2,1,0:T(8,128)(2,1)}, bf16[8,160,768]{2,1,0:T(8,128)(2,1)}, u32[]{:S(2)}, u32[]{:S(2)}) collective-permute-start(bf16[8,160,768]{2,1,0:T(8,128)(2,1)} %get-tuple-element.144), channel_id=1, source_target_pairs={{0,1},{1,0},{2,3},{3,2},{4,5},{5,4},{6,7},{7,6},{8,9},{9,8},{10,11... | collective-permute-start | bytes 5898248 | tf_op jit(solution)/shard_map/ppermute | solution.py:674
  175.5 13.8 %collective-permute-start.14 = (bf16[2,144,768]{2,1,0:T(8,128)(2,1)}, bf16[2,144,768]{2,1,0:T(8,128)(2,1)}, u32[]{:S(2)}, u32[]{:S(2)}) collective-permute-start(bf16[2,144,768]{2,1,0:T(8,128)(2,1)} %fusion.7), channel_id=1, source_target_pairs={{0,2},{1,3},{2,0},{3,1},{4,6},{5,7},{6,4},{7,5},{8,10},{9,11},{10,... | collective-permute-start | bytes 1327112 | tf_op jit(solution)/shard_map/ppermute | solution.py:674
  178.0 11.3 %collective-permute-start.13 = (bf16[2,128,768]{2,1,0:T(8,128)(2,1)}, bf16[2,128,768]{2,1,0:T(8,128)(2,1)}, u32[]{:S(2)}, u32[]{:S(2)}) collective-permute-start(bf16[2,128,768]{2,1,0:T(8,128)(2,1)} %fusion.11), channel_id=1, source_target_pairs={{0,4},{1,5},{2,6},{3,7},{4,0},{5,1},{6,2},{7,3},{8,12},{9,13},{10,... | collective-permute-start | bytes 1179656 | tf_op jit(solution)/shard_map/ppermute | solution.py:674
  191.6 22.2 %collective-permute-start.15 = (bf16[2,2,96,768]{3,2,1,0:T(8,128)(2,1)}, bf16[2,2,96,768]{3,2,1,0:T(8,128)(2,1)}, u32[]{:S(2)}, u32[]{:S(2)}) collective-permute-start(bf16[2,2,96,768]{3,2,1,0:T(8,128)(2,1)} %fusion.12), channel_id=1, source_target_pairs={{0,2},{1,3},{2,0},{3,1},{4,6},{5,7},{6,4},{7,5},{8,10},{9,11},{10,... | collective-permute-start | bytes 1769480 | tf_op jit(solution)/shard_map/ppermute | solution.py:674
  195.2 18.6 %collective-permute-start.16 = (bf16[2,2,64,768]{3,2,1,0:T(8,128)(2,1)}, bf16[2,2,64,768]{3,2,1,0:T(8,128)(2,1)}, u32[]{:S(2)}, u32[]{:S(2)}) collective-permute-start(bf16[2,2,64,768]{3,2,1,0:T(8,128)(2,1)} %fusion.30), channel_id=1, source_target_pairs={{0,4},{1,5},{2,6},{3,7},{4,0},{5,1},{6,2},{7,3},{8,12},{9,13},{10,... | collective-permute-start | bytes 1179656 | tf_op jit(solution)/shard_map/ppermute | solution.py:674
  196.7 16.2 %collective-permute-start.17 = (bf16[192,768]{1,0:T(8,128)(2,1)}, bf16[192,768]{1,0:T(8,128)(2,1)S(1)}, u32[]{:S(2)}, u32[]{:S(2)}) collective-permute-start(bf16[192,768]{1,0:T(8,128)(2,1)} %pad_maximum_fusion.2), channel_id=1, source_target_pairs={{0,8},{1,9},{2,10},{3,11},{4,12},{5,13},{6,14},{7,15},{8,0},{9,1},... | collective-permute-start | bytes 884744 | tf_op jit(solution)/shard_map/ppermute | solution.py:674
  200.6 24.5 %copy-start.14 = (bf16[2,96,768]{2,1,0:T(8,128)(2,1)S(1)}, bf16[2,96,768]{2,1,0:T(8,128)(2,1)}, u32[]{:S(2)}) copy-start(bf16[2,96,768]{2,1,0:T(8,128)(2,1)} %copy-done.13) | copy-start | bytes 884740
  202.0 31.9 %collective-permute-start.21 = (bf16[272,768]{1,0:T(8,128)(2,1)S(1)}, bf16[272,768]{1,0:T(8,128)(2,1)S(1)}, u32[]{:S(2)}, u32[]{:S(2)}) collective-permute-start(bf16[272,768]{1,0:T(8,128)(2,1)S(1)} %pad_maximum_fusion.1), channel_id=1, source_target_pairs={{0,8},{1,9},{2,10},{3,11},{4,12},{5,13},{6,14},{7,15},{8,0},{9,1},... | collective-permute-start | bytes 1253384 | tf_op jit(solution)/shard_map/ppermute | solution.py:674
  215.1 17.5 %collective-permute-start.19 = (bf16[2,96,768]{2,1,0:T(8,128)(2,1)S(1)}, bf16[2,96,768]{2,1,0:T(8,128)(2,1)S(1)}, u32[]{:S(2)}, u32[]{:S(2)}) collective-permute-start(bf16[2,96,768]{2,1,0:T(8,128)(2,1)S(1)} %fusion.20), channel_id=1, source_target_pairs={{0,4},{1,5},{2,6},{3,7},{4,0},{5,1},{6,2},{7,3},{8,12},{9,13},{10,... | collective-permute-start | bytes 884744 | tf_op jit(solution)/shard_map/ppermute | solution.py:674
  224.6 5.7 %collective-permute-start.18 = (bf16[2,64,768]{2,1,0:T(8,128)(2,1)S(1)}, bf16[2,64,768]{2,1,0:T(8,128)(2,1)S(1)}, u32[]{:S(2)}, u32[]{:S(2)}) collective-permute-start(bf16[2,64,768]{2,1,0:T(8,128)(2,1)S(1)} %fusion.32), channel_id=1, source_target_pairs={{0,2},{1,3},{2,0},{3,1},{4,6},{5,7},{6,4},{7,5},{8,10},{9,11},{10,... | collective-permute-start | bytes 589832 | tf_op jit(solution)/shard_map/ppermute | solution.py:674
  230.3 6.3 %copy-start.17 = (bf16[2,64,768]{2,1,0:T(8,128)(2,1)}, bf16[2,64,768]{2,1,0:T(8,128)(2,1)S(1)}, u32[]{:S(2)}) copy-start(bf16[2,64,768]{2,1,0:T(8,128)(2,1)S(1)} %collective-permute-done.18) | copy-start | bytes 589828
  232.7 3.9 %copy-start.15 = (bf16[2,96,768]{2,1,0:T(8,128)(2,1)}, bf16[2,96,768]{2,1,0:T(8,128)(2,1)S(1)}, u32[]{:S(2)}) copy-start(bf16[2,96,768]{2,1,0:T(8,128)(2,1)S(1)} %collective-permute-done.19) | copy-start | bytes 884740
  236.6 9.6 %copy-start.18 = (bf16[2,64,768]{2,1,0:T(8,128)(2,1)S(1)}, bf16[2,64,768]{2,1,0:T(8,128)(2,1)}, u32[]{:S(2)}) copy-start(bf16[2,64,768]{2,1,0:T(8,128)(2,1)} %copy-done.17) | copy-start | bytes 589828
  236.6 10.7 %copy-start.16 = (bf16[2,96,768]{2,1,0:T(8,128)(2,1)S(1)}, bf16[2,96,768]{2,1,0:T(8,128)(2,1)}, u32[]{:S(2)}) copy-start(bf16[2,96,768]{2,1,0:T(8,128)(2,1)} %copy-done.15) | copy-start | bytes 884740
  236.7 9.5 %collective-permute-start.20 = (bf16[160,768]{1,0:T(8,128)(2,1)S(1)}, bf16[160,768]{1,0:T(8,128)(2,1)S(1)}, u32[]{:S(2)}, u32[]{:S(2)}) collective-permute-start(bf16[160,768]{1,0:T(8,128)(2,1)S(1)} %pad_maximum_fusion.3), channel_id=1, source_target_pairs={{0,8},{1,9},{2,10},{3,11},{4,12},{5,13},{6,14},{7,15},{8,0},{9,1},... | collective-permute-start | bytes 737288 | tf_op jit(solution)/shard_map/ppermute | solution.py:674
  241.9 7.9 %copy-start.1 = (bf16[1,128,2304]{2,1,0:T(8,128)(2,1)S(1)}, bf16[1,128,2304]{2,1,0:T(8,128)(2,1)}, u32[]{:S(2)}) copy-start(bf16[1,128,2304]{2,1,0:T(8,128)(2,1)} %param.19) | copy-start | bytes 1769476
where the time goes:
time: 253 us; the launch traced here: 250 us
  Pallas kernels  107 us (42%)
  waiting for transfers between devices  63.7 us (25%)
  other arithmetic  38.1 us (15%)
  starting transfers between devices  32.4 us (13%)
  local copies, waits for them, and re-layouts  7.1 us (3%)
    pallas_call x8, Pallas kernels, stage(): pl.pallas_call(partial(stage_kernel, common.sizes, parts, term, who, slot...  107 us
    ppermute x18, waiting for transfers between devices, exchange(): return lax.ppermute(block, axis, [(i, i ^ 1 << bit) for i in range(count)])  42.7 us
    ppermute x18, starting transfers between devices, exchange(): return lax.ppermute(block, axis, [(i, i ^ 1 << bit) for i in range(count)])  27.2 us
    convert_element_type x16, other arithmetic, split(): sum((self.take(term, start, left, bit) for term, left, start in self.terms))  26.3 us
    ppermute x4, waiting for transfers between devices, per_device(): over = lambda block, route: lax.ppermute(block, 'section', route)  21 us
    add x5, other arithmetic, total(): sum((self.take(term, start, left, None) for term, left, start in self.ter...  6.18 us
    ppermute x4, starting transfers between devices, per_device(): over = lambda block, route: lax.ppermute(block, 'section', route)  5.21 us
  transfers between devices with their start and end apart: 22, of which 11 were waited for; matrix products, arithmetic and copies ran while one was open for 10% of the time, Pallas kernels for 35%

commit v1 on v0

v1 whole, which is shorter than its diff:
```python
from functools import partial
import inspect
import math

import jax
import jax.numpy as jnp
import numpy as np
from jax import lax
from jax.experimental import pallas as pl
from jax.experimental.pallas import tpu as pltpu
from jax.sharding import PartitionSpec as P

HEADS = 12
HEAD = 64
EMB = 128
SEGS = 4
ANY = pl.ANY
VMEM = pltpu.MemorySpace.VMEM
SMEM = pltpu.MemorySpace.SMEM
F32 = jnp.float32
BF16 = jnp.bfloat16
ROOT_HALF = 0.7071067811865476
ROOT_TAU = 0.3989422804014327
TILE = 384
TAIL_ROWS = 24
GAIN_ROWS = 16
EXTRA = 16


class Bag(dict):
    __getattr__ = dict.__getitem__


def dot(left, right, left_dim=1, right_dim=0):
    return lax.dot_general(
        left, right, (((left_dim,), (right_dim,)), ((), ())), preferred_element_type=F32
    )


def repeat(count, body):
    for i in range(count):
        body(i)


def steps_of(count, size, body):
    def several(i, _):
        for j in range(size):
            body(size * i + j)
        return _

    lax.fori_loop(0, count // size, several, 0)


def lanes(index, size, start=0):
    if isinstance(index, int):
        return slice(start + index * size, start + (index + 1) * size)
    return pl.ds(pl.multiple_of(start + index * size, size), size)


def swap_halves(values, low_half):
    forth = pltpu.roll(values, 128 - HEAD // 2, 1)
    back = pltpu.roll(values, HEAD // 2, 1)
    return jnp.where(low_half, forth, back)


def norm_parts(values):
    center = values - jnp.mean(values, axis=-1, keepdims=True)
    spread = jnp.mean(center * center, axis=-1, keepdims=True)
    factor = lax.rsqrt(spread + 1e-05)
    return center * factor, factor


def norm_back(grad, unit, factor):
    return factor * (
        grad
        - jnp.mean(grad, axis=-1, keepdims=True)
        - unit * jnp.mean(grad * unit, axis=-1, keepdims=True)
    )


class Held:
    def __init__(self, bufs, loads, stores, sems):
        self.bufs = bufs
        self.loads = loads
        self.stores = stores
        self.sems = sems
        self.names = {id(buf): name for name, buf in bufs.items()}
        self.spots = {name: n for n, name in enumerate(loads)}
        self.pending = set(loads)
        self.waiting = set(loads)
        self.leaving = {}

    def load(self, name):
        return pltpu.make_async_copy(
            self.loads[name], self.bufs[name], self.sems.at[self.spots[name]]
        )

    def store(self, name, at):
        number, _ = self.leaving[(name, at)]
        source, target = self.bufs[name], self.stores[name]
        if at is not None:
            spot = tuple(pl.ds(*item) for item in at)
            source, target = source.at[spot], target.at[spot]
        return pltpu.make_async_copy(source, target, self.sems.at[number])

    def begin(self, *bufs):
        for buf in bufs:
            name = self.names[id(buf)]
            if name in self.waiting:
                self.waiting.remove(name)
                self.load(name).start()

    def begin_all(self):
        self.begin(*[self.bufs[name] for name in self.loads])

    def need(self, *bufs):
        self.begin(*bufs)
        for buf in bufs:
            name = self.names[id(buf)]
            if name in self.pending:
                self.pending.remove(name)
                self.load(name).wait()

    def done(self, *bufs, at=None):
        for buf in bufs:
            name = self.names[id(buf)]
            if name in self.stores:
                self.leaving[(name, at)] = (len(self.loads) + len(self.leaving), at)
                self.store(name, at).start()

    def finish(self):
        for name, at in self.leaving:
            self.store(name, at).wait()


class Layer:
    def __init__(self, sizes, slot, refs):
        self.span, self.width, self.hidden, self.count = sizes
        self.slot = slot
        lengths, section, self.mods, self.trig, self.gain, self.ebias, self.rbias = refs
        self.section = section[0]
        self.single = lengths[slot, 0] == self.span
        self.pairs = self.width // 128
        self.seg = self.span // SEGS
        self.step = self.width
        self.tiles = self.hidden // self.step
        place = lax.broadcasted_iota(jnp.int32, (self.span, 128), 1)
        self.low_half = place % HEAD < HEAD // 2
        self.low_head = place < HEAD
        row = lax.broadcasted_iota(jnp.int32, (1, 128), 1) // HEAD
        self.head_row = [(row == i).astype(F32).astype(BF16) for i in range(2)]
        self.blocks = [(b, slice(b * self.seg, (b + 1) * self.seg)) for b in range(SEGS)]

    def trig_pair(self):
        cos_all, sin_all = self.trig[0], self.trig[1]
        cos_cut = jnp.concatenate([cos_all[: self.seg]] * SEGS, axis=0)
        sin_cut = jnp.concatenate([sin_all[: self.seg]] * SEGS, axis=0)
        return jnp.where(self.single, cos_all, cos_cut), jnp.where(self.single, sin_all, sin_cut)

    def mod_row(self, block, part):
        row = self.slot * SEGS + jnp.where(self.single, 0, block)
        return self.mods[pl.ds(row, 1), part * self.width : (part + 1) * self.width]

    def add_segment(self, small, block, at, sums):
        row = 2 + jnp.where(self.single, 0, block)
        small[pl.ds(row, 1), at * self.width : (at + 1) * self.width] += sums

    def put_left(self, left, base, first, values):
        turned = values.T
        lines = (self.hidden if base == 0 else self.width) // self.count
        if left.shape[0] == 1:
            left[0, 2 * base + first : 2 * base + first + turned.shape[0]] = turned
            return
        for block in range(first // lines, (first + turned.shape[0]) // lines):
            at = block * lines - first
            to = base + block // 2 * lines
            left[block % 2, to : to + lines] = turned[at : at + lines]

    def thirds(self, index):
        return [lanes(index, 128, p * self.width) for p in range(3)]


def left_bases(width, hidden):
    return 0, hidden // 2, (hidden + width) // 2, (hidden + 2 * width) // 2


def forward(
    k, xv, win, wout, wex, wre, left, qkv, probs, middle, slope, branch, result, bias, normed,
    mixed, modded,
):
    span, width, held = k.span, k.width, k.held
    at_active, at_modded, at_mixed, at_normed = left_bases(width, k.hidden)
    held.begin(xv, win)
    held.need(xv)
    unit, _ = norm_parts(xv[...].astype(F32))
    normed[...] = (unit * k.gain[...].astype(F32)).astype(BF16)
    across = lax.broadcasted_iota(jnp.int32, (span, span), 0) // k.seg
    down = lax.broadcasted_iota(jnp.int32, (span, span), 1) // k.seg
    bias[...] = jnp.where((across == down) | k.single, 0.0, -1e30)
    held.need(win)
    held.begin(wout, wex, wre)
    cos_part, sin_part = k.trig_pair()
    for tile, factor in ((0, 0.125), (1, 1.0)):
        for i in range(width // 256):
            at = lanes(i, 256, tile * width)
            joint = dot(normed[...], win[:, at])
            outs = []
            for piece in (joint[:, :128], joint[:, 128:]):
                turned = piece * cos_part + swap_halves(piece, k.low_half) * sin_part
                outs.append((turned * factor).astype(BF16))
            qkv[:, at] = jnp.concatenate(outs, axis=1)
    qkv[:, 2 * width :] = dot(normed[...], win[:, 2 * width :]).astype(BF16)
    held.done(qkv)
    if k.kept:
        k.put_left(left, at_normed, 0, normed[...])

    def heads(i):
        at = k.thirds(i)
        query, key, value = (qkv[:, a] for a in at)
        outs = []
        for h in range(2):
            scores = dot(key * k.head_row[h], query, 1, 1) + bias[...]
            top = jnp.max(scores, axis=0, keepdims=True)
            raised = jnp.exp(scores - top)
            total = jnp.sum(raised, axis=0, keepdims=True)
            prob = raised * (1.0 / total)
            if k.kept:
                probs[2 * i + h] = prob
            outs.append(dot(prob.astype(BF16), value, 0, 0))
        mixed[:, at[0]] = jnp.where(k.low_head, outs[0], outs[1]).astype(BF16)

    steps_of(k.pairs, k.heads_step, heads)
    held.done(probs)
    held.need(wout)
    middle[...] = xv[...].astype(F32) + dot(mixed[...], wout[...])
    held.done(middle)
    if k.kept:
        k.put_left(left, at_mixed, 0, mixed[...])
    for b, rows in k.blocks:
        unit, _ = norm_parts(middle[rows])
        modded[rows] = (unit * (1.0 + k.mod_row(b, 0)) + k.mod_row(b, 1)).astype(BF16)
    if k.kept:
        k.put_left(left, at_modded, 0, modded[...])
    held.need(wex, wre)
    branch[...] = jnp.broadcast_to(k.rbias[...].astype(F32), (span, width))

    def feed(j):
        at = lanes(j, k.step)
        pre = dot(modded[...], wex[:, at]) + k.ebias[:, at].astype(F32)
        area = 0.5 + 0.5 * lax.erf(pre * ROOT_HALF)
        out = (pre * area).astype(BF16)
        if k.kept:
            slope[:, at] = area + pre * (jnp.exp(pre * pre * -0.5) * ROOT_TAU)
            k.put_left(left, at_active, j * k.step, out)
        branch[...] += dot(out, wre[at, :])

    repeat(k.tiles, feed)
    held.done(slope, left, branch)
    for b, rows in k.blocks:
        result[rows] = (middle[rows] + k.mod_row(b, 2) * branch[rows]).astype(BF16)
    held.done(result)


def output(k, dyv, bg):
    k.held.need(dyv)
    for b, rows in k.blocks:
        bg[rows] = (dyv[rows].astype(F32) * k.mod_row(b, 2)).astype(BF16)
    k.held.done(bg)


def mlp(k, wre, wex, bg, slope, middle, branch, dyv, pa, middle_grad, small, acc):
    span, width, hidden, held = k.span, k.width, k.hidden, k.held
    small[...] = jnp.zeros(small.shape, F32)
    acc[...] = jnp.zeros(acc.shape, F32)
    held.need(bg, wre, slope)
    held.begin(wex, middle, dyv, branch)
    held.need(wex)

    def feed(j):
        at = lanes(j, k.step)
        grad = dot(bg[...], wre[at, :], 1, 1)
        pre_grad = (slope[:, at] * grad).astype(BF16)
        pa[:span, at] = pre_grad
        small[0:1, at] = jnp.sum(pre_grad.astype(F32), axis=0, keepdims=True)
        acc[...] += dot(pre_grad, wex[:, at], 1, 1)

    repeat(k.tiles, feed)
    held.need(middle, dyv, branch)
    total = jnp.zeros((1, width), F32)
    for b, rows in k.blocks:
        cotan = dyv[rows].astype(F32)
        total += jnp.sum(bg[rows].astype(F32), axis=0, keepdims=True)
        grad = acc[rows]
        unit, factor = norm_parts(middle[rows])
        k.add_segment(small, b, 0, jnp.sum(grad * unit, axis=0, keepdims=True))
        k.add_segment(small, b, 1, jnp.sum(grad, axis=0, keepdims=True))
        k.add_segment(small, b, 2, jnp.sum(cotan * branch[rows], axis=0, keepdims=True))
        back = norm_back(grad * (1.0 + k.mod_row(b, 0)), unit, factor)
        full = cotan + back
        middle_grad[rows] = full
        pa[rows, hidden:] = full.astype(BF16)
    small[1:2, :width] = total
    pa[span:, :] = small[...].astype(BF16)
    held.done(pa, middle_grad)


def attend(
    k, wout, win, agrad, probs, qkv, xv, middle_grad, jg, leave, mixed_grad, acc
):
    span, held = k.span, k.held
    held.need(agrad, wout)
    held.begin(probs, qkv)
    mixed_grad[...] = dot(agrad[...], wout[...], 1, 1).astype(BF16)
    held.need(probs, qkv)
    held.begin(win, xv, middle_grad)
    cos_part, sin_part = k.trig_pair()

    def heads(i):
        at = k.thirds(i)
        query, key, value = (qkv[:, a] for a in at)
        out_grad = mixed_grad[:, at[0]]
        parts = []
        for h in range(2):
            prob = probs[2 * i + h]
            pull = dot(value * k.head_row[h], out_grad, 1, 1)
            shared = jnp.sum(prob * pull, axis=0, keepdims=True)
            score_grad = (prob * (pull - shared)).astype(BF16)
            parts.append(
                (
                    dot(score_grad, key, 0, 0),
                    dot(score_grad, query),
                    dot(prob.astype(BF16), out_grad),
                )
            )
        for p in range(3):
            grad = jnp.where(k.low_head, parts[0][p], parts[1][p])
            if p < 2:
                grad = grad * cos_part - swap_halves(grad, k.low_half) * sin_part
                if p == 0:
                    grad = grad * 0.125
            jg[:span, at[p]] = grad.astype(BF16)

    steps_of(k.pairs, k.heads_step, heads)
    held.need(win, xv, middle_grad)
    acc[...] = dot(jg[:span, :], win[...], 1, 1)
    total = jnp.zeros((1, k.width), F32)
    for b, rows in k.blocks:
        grad = acc[rows]
        unit, factor = norm_parts(xv[rows].astype(F32))
        total += jnp.sum(grad * unit, axis=0, keepdims=True)
        back = norm_back(grad * k.gain[...].astype(F32), unit, factor)
        leave[rows] = (middle_grad[rows] + back).astype(BF16)
    below = jnp.concatenate([total, jnp.zeros((EXTRA - 1, k.width), F32)], axis=0)
    jg[span:, : k.width] = below.astype(BF16)
    jg[span:, k.width :] = jnp.zeros((EXTRA, 2 * k.width), BF16)
    held.done(jg, leave)


def copy_agrad(k, pa, agrad):
    agrad[...] = pa[: k.span, k.hidden :]


class Sums:
    def __init__(self, ranks, full, outs, sems):
        self.full = full
        self.own = [((ranks[0] >> bit) & 1) == 0 for bit in (1, 2)]
        self.bufs = outs[:4]
        self.targets = outs[4:]
        self.sems = sems
        self.half = full.shape[1] // 2
        self.copies = []

    def put(self, block, at, values):
        self.full[block, at] = values

    def settle(self, which, groups):
        send, keep = self.bufs[2 * which : 2 * which + 2]
        at = slice(which * self.half, (which + 1) * self.half)
        apart = 1 + which
        for group in groups:
            for n in range(2):
                first = 4 * group + (2 * n if which == 0 else n)
                even, odd = self.full[first, at], self.full[first + apart, at]
                send[2 * group + n] = jnp.where(self.own[which], odd, even).astype(BF16)
                keep[2 * group + n] = jnp.where(self.own[which], even, odd)
            spot = pl.ds(2 * group, 2)
            for n in range(2 * which, 2 * which + 2):
                copy = pltpu.make_async_copy(
                    self.bufs[n].at[spot], self.targets[n].at[spot], self.sems.at[len(self.copies)]
                )
                copy.start()
                self.copies.append(copy)

    def finish(self):
        for copy in self.copies:
            copy.wait()


def term_reduce(k, sums, left, right):
    lines = k.hidden // k.count
    per = TILE // lines
    for tile in range(k.hidden // 2 // TILE):
        total = dot(left[tile * TILE : (tile + 1) * TILE], right[...])
        for n in range(per):
            sums.put(tile * per + n, slice(0, lines), total[n * lines : (n + 1) * lines])
        if (tile + 1) * per % 4 == 0:
            group = ((tile + 1) * per // 4 - 1,)
            sums.settle(0, group)
            sums.settle(1, group)


def square_terms(k, sums, left, right, cols, part):
    lines = k.width // k.count
    total = dot(left, right[: 4 * k.span, cols])
    for n in range(k.count // 2):
        sums.put(n, slice(part * lines, (part + 1) * lines), total[n * lines : (n + 1) * lines])


def term_expand(k, sums, left, right):
    width, hidden, span = k.width, k.hidden, k.span
    groups = range(k.count // 8)
    tall = hidden // width
    lines = width // k.count
    rows = width // 2
    half = sums.half
    settled = False
    for col in range(tall + 1):
        part = left[:rows] if col < tall else left[rows:]
        square_terms(k, sums, part, right, slice(col * width, (col + 1) * width), col)
        if (col + 1) * lines >= half and not settled:
            sums.settle(0, groups)
            settled = True
    smalls = [k.small[n].astype(F32) for n in range(4)]
    times = sum(
        k.embeds[n // 2][:, n % 2 * SEGS + s : n % 2 * SEGS + s + 1]
        * smalls[n][2 + s : 3 + s, : 3 * width]
        for n in range(4)
        for s in range(SEGS)
    )
    both = sum(smalls)
    seq_sum = jnp.sum(both[2 : 2 + SEGS, : 3 * width], axis=0, keepdims=True)
    lines_v = k.lines
    lines_v[...] = jnp.zeros(lines_v.shape, F32)
    lines_v[0:1] = both[1:2, :width]
    for n in range(3):
        lines_v[1 + n : 2 + n] = seq_sum[:, n * width : (n + 1) * width]
    for n in range(tall):
        lines_v[4 + n : 5 + n] = both[0:1, n * width : (n + 1) * width]
    deep = EMB // k.count
    first = (tall + 1) * lines
    for g in range(k.count // 2):
        for side in range(2):

            @pl.when(k.core == side)
            def _(at=(2 * g + side) * deep, g=g):
                for p in range(3):
                    to = first + p * deep
                    piece = times[at : at + deep, p * width : (p + 1) * width]
                    sums.put(g, slice(to, to + deep), piece)

        sums.put(g, slice(first + 3 * deep, 2 * half), lines_v[...])
    sums.settle(1, groups)


def term_attend(k, sums, left, right):
    width = k.width
    groups = range(k.count // 8)
    lines = width // k.count
    settled = False
    for col in range(3):
        square_terms(k, sums, left[...], right, slice(col * width, (col + 1) * width), col)
        if (col + 1) * lines >= sums.half and not settled:
            sums.settle(0, groups)
            settled = True
    gain = sum(k.small[n].astype(F32) for n in range(4))[:, :width]
    for g in range(k.count // 2):
        sums.put(g, slice(3 * lines, 3 * lines + GAIN_ROWS), gain)
    sums.settle(1, groups)


def load_terms(k, refs, bufs, base, sems):
    left_v, right_v, small_v = bufs
    copies = []
    rows = left_v.shape[0]
    for n, (left, right) in enumerate(zip(refs[:4], refs[4:8])):
        source = left.at[k.core] if n < 2 else left
        tokens = pl.ds(n * k.span, k.span)
        copies.append((source.at[pl.ds(base, rows)], left_v.at[:, tokens]))
        copies.append((right.at[pl.ds(0, k.span)], right_v.at[tokens]))
        if small_v is not None:
            copies.append((right.at[pl.ds(k.span, EXTRA)], small_v.at[n]))
    made = [pltpu.make_async_copy(*pair, sems.at[n]) for n, pair in enumerate(copies)]
    for copy in made:
        copy.start()
    return made


class Terms:
    def __init__(self, sizes, core):
        self.span, self.width, self.hidden, self.count = sizes
        self.core = core[0]


def term_kernel(sizes, body, base, extra, *refs):
    refs = list(refs)
    core, rank = refs[:2]
    k = Terms(sizes, core)
    pos = 2
    if body is term_expand:
        k.embeds = refs[pos : pos + 2]
        pos += 2
    sources = refs[pos : pos + 8]
    pos += 8 + extra
    targets = refs[pos : pos + 4]
    pos += 4
    left_v, right_v, full, *outs = refs[pos : pos + 7]
    pos += 7
    k.small = None
    if body is not term_reduce:
        k.small, k.lines = refs[pos : pos + 2]
        pos += 2
    sems, out_sems = refs[pos:]
    copies = load_terms(k, sources, (left_v, right_v, k.small), base, sems)
    sums = Sums(rank, full, outs + targets, out_sems)
    for copy in copies:
        copy.wait()
    body(k, sums, left_v, right_v)
    sums.finish()


def term_call(name, body, sizes, lines, base, rows, core, rank, lefts, rights, embeds=(), after=()):
    span, width, hidden, count = sizes
    blocks = count // 2
    cols = rights[0].shape[1]
    half = lines // 2
    outs = [((blocks // 2, half, width), kind) for kind in (BF16, F32)] * 2
    scratch = [
        ((rows, 4 * span), BF16),
        ((4 * span, cols), BF16),
        ((blocks, lines, width), F32),
        *outs,
    ]
    if body is not term_reduce:
        scratch += [((4, EXTRA, cols), BF16), ((TAIL_ROWS, width), F32)]
    args = [core.reshape(1), rank.reshape(1), *embeds, *lefts, *rights, *after]
    in_specs = [pl.BlockSpec(memory_space=SMEM)] * 2
    in_specs += [pl.BlockSpec(memory_space=VMEM)] * len(embeds)
    in_specs += [pl.BlockSpec(memory_space=ANY)] * (8 + len(after))
    return pl.pallas_call(
        partial(term_kernel, sizes, body, base, len(after)),
        out_shape=[jax.ShapeDtypeStruct(*item) for item in outs],
        in_specs=in_specs,
        out_specs=[pl.BlockSpec(memory_space=ANY)] * 4,
        scratch_shapes=[pltpu.VMEM(*item) for item in scratch]
        + [pltpu.SemaphoreType.DMA((12,)), pltpu.SemaphoreType.DMA((8,))],
        compiler_params=pltpu.CompilerParams(vmem_limit_bytes=56 * 1024 * 1024),
        name=name,
    )(*args)


def plain_pieces(lefts, rights, embed, sizes):
    span, width, hidden, count = sizes
    bg, pa, jg = rights
    bases = [2 * base for base in left_bases(width, hidden)]

    def blocks(base, rows, right):
        total = sum(dot(a[0, base : base + rows], b) for a, b in zip(lefts, right))
        parts = [total[:, i : i + width] for i in range(0, total.shape[1], width)]
        return [part.reshape(count, -1, width) for part in parts]

    take = lambda items, cols: [item[:span, cols] for item in items]
    reduce = blocks(bases[0], hidden, bg)
    expand = blocks(bases[1], width, take(pa, slice(0, hidden)))
    expand += blocks(bases[2], width, take(pa, slice(hidden, hidden + width)))
    last = blocks(bases[3], width, take(jg, slice(None)))
    small = [item[span:].astype(F32) for item in pa]
    seqs = jnp.concatenate([item[2 : 2 + SEGS, : 3 * width] for item in small])
    times = jnp.dot(embed, seqs, precision=lax.Precision.HIGHEST)
    expand += [times[:, i * width : (i + 1) * width].reshape(count, -1, width) for i in range(3)]
    lines = jnp.concatenate(
        [
            sum(item[1:2, :width] for item in small),
            jnp.sum(seqs, axis=0).reshape(-1, width),
            sum(item[0, :hidden] for item in small).reshape(-1, width),
        ]
    )
    lines = jnp.pad(lines, ((0, TAIL_ROWS - lines.shape[0]), (0, 0)))
    gain = sum(item[span:, :width].astype(F32) for item in jg)
    expand.append(jnp.broadcast_to(lines, (count,) + lines.shape))
    last.append(jnp.broadcast_to(gain, (count,) + gain.shape))
    return [jnp.concatenate(item, axis=1) for item in (reduce, expand, last)]


def shapes_of(span, width, hidden, cores):
    tok = lambda cols, kind=BF16: ((span, cols), kind)
    below = lambda cols: ((span + EXTRA, cols), BF16)
    return dict(
        xv=tok(width),
        dyv=tok(width),
        win=((width, 3 * width), BF16),
        wout=((width, width), BF16),
        wex=((width, hidden), BF16),
        wre=((hidden, width), BF16),
        left=((cores, (hidden + 3 * width) // cores, span), BF16),
        normed=tok(width),
        qkv=tok(3 * width),
        probs=((HEADS, span, span), F32),
        mixed=tok(width),
        middle=tok(width, F32),
        modded=tok(width),
        slope=tok(hidden, F32),
        branch=tok(width, F32),
        result=tok(width),
        bg=tok(width),
        pa=below(hidden + width),
        jg=below(3 * width),
        agrad=tok(width),
        mixed_grad=tok(width),
        middle_grad=tok(width, F32),
        leave=tok(width),
        acc=tok(width, F32),
        bias=tok(span, F32),
        small=((EXTRA, hidden + width), F32),
    )


def uses(part):
    return list(inspect.signature(part).parameters)[1:]


def stage_kernel(sizes, parts, who, slot, plan, *refs):
    refs = list(refs)
    layer = Layer(sizes, slot, refs[:7])
    span = layer.span
    pos = 7
    loads = {}
    for name, row, cols in plan.sources:
        ref = refs[pos]
        if cols is not None:
            ref = ref.at[pl.ds(0, span), pl.ds(*cols)]
        elif row is not None:
            ref = ref.at[pl.ds(row, span)]
        loads[name] = ref
        pos += 1
    pos += plan.extra
    stores = {}
    for name, row in plan.targets:
        stores[name] = refs[pos] if row is None else refs[pos].at[pl.ds(row, span)]
        pos += 1
    bufs = {}
    for name in plan.bufs:
        bufs[name] = refs[pos]
        pos += 1
    layer.held = Held(bufs, loads, stores, refs[pos])
    layer.kept = plan.kept
    layer.heads_step = plan.heads_step

    @pl.when(layer.section == who)
    def _():
        for part in parts:
            part(layer, *[bufs[name] for name in uses(part)])
        layer.held.finish()


def stage(
    name, common, parts, who, slot, loads, stores, carried=None, after=(), kept=True, heads_step=3
):
    carried = carried or {}
    span, width, hidden, count = common.sizes
    shapes = shapes_of(span, width, hidden, common.cores)
    bufs = []
    for part in parts:
        bufs += [item for item in uses(part) if item not in bufs]
    pair = lambda item: item if isinstance(item, tuple) else (item, None)
    args = list(common.args)
    in_specs = [pl.BlockSpec(memory_space=SMEM)] * 2 + [pl.BlockSpec(memory_space=VMEM)] * 5
    plan = Bag(sources=[], targets=[], bufs=bufs, kept=kept, heads_step=heads_step)
    for item in loads:
        if item in bufs:
            array, row, *cols = pair(loads[item])
            args.append(array)
            plan.sources.append((item, row, cols[0] if cols else None))
    outs, aliases, extra = [], {}, []
    targets = [(item, *pair(key)) for item, key in stores.items()]
    for i, (item, key, row) in enumerate(targets):
        shape, kind = shapes[item]
        if row is not None:
            shape = (common.tokens,) + shape[1:]
        outs.append(jax.ShapeDtypeStruct(shape, kind))
        plan.targets.append((item, row))
        if key in carried:
            aliases[len(args) + len(extra)] = i
            extra.append(carried[key])
    extra += list(after)
    args += extra
    plan["extra"] = len(extra)
    in_specs += [pl.BlockSpec(memory_space=ANY)] * (len(args) - len(in_specs))
    results = pl.pallas_call(
        partial(stage_kernel, common.sizes, parts, who, slot, plan),
        out_shape=outs,
        in_specs=in_specs,
        out_specs=[pl.BlockSpec(memory_space=ANY)] * len(outs),
        input_output_aliases=aliases,
        scratch_shapes=[pltpu.VMEM(*shapes[item]) for item in bufs]
        + [pltpu.SemaphoreType.DMA((32,))],
        compiler_params=pltpu.CompilerParams(vmem_limit_bytes=56 * 1024 * 1024),
        name=name,
    )(*args)
    return Bag({key: value for (_, key, _), value in zip(targets, results)})


def bits_of(count):
    bits = count.bit_length() - 1
    assert 1 << bits == count
    return bits


class Chunk:
    def __init__(self, axis, bits, size, settled=()):
        self.axis = axis
        self.bits = list(range(bits - 1, 0, -1))
        self.size = size
        self.settled = list(settled)
        self.terms = []

    def add(self, term, start=0):
        left = [bit for bit in self.bits if bit not in self.settled]
        self.terms.append((term.reshape((2,) * len(left) + term.shape[-2:]), left, start))

    def take(self, term, start, left, flip):
        me = lax.axis_index(self.axis)
        side = lambda bit: 1 - ((me >> bit) & 1) if bit == flip else (me >> bit) & 1
        starts = [side(bit) if bit in self.settled else 0 for bit in left]
        sizes = [1 if bit in self.settled else 2 for bit in left]
        cols = term.shape[-1]
        piece = lax.dynamic_slice(term, starts + [start, 0], sizes + [self.size, cols])
        open_bits = [2] * (len(self.bits) - len(self.settled))
        return piece.reshape(open_bits + [self.size, cols]).astype(F32)

    def split(self, bit):
        self.settled.append(bit)
        return sum(self.take(term, start, left, bit) for term, left, start in self.terms).astype(
            BF16
        )

    def total(self):
        return sum(self.take(term, start, left, None) for term, left, start in self.terms)


def exchange(block, axis, bit):
    count = lax.axis_size(axis)
    return lax.ppermute(block, axis, [(i, i ^ (1 << bit)) for i in range(count)])


def join(*items):
    return lax.optimization_barrier(items)


def angle_table(span):
    half = HEAD // 2
    freqs = np.exp(-math.log(10000.0) * np.arange(half, dtype=np.float32) / half)
    phase = np.arange(span, dtype=np.float32)[:, None] * freqs.astype(np.float32)[None, :]
    cos_part, sin_part = np.cos(phase), np.sin(phase)
    return np.stack(
        [
            np.concatenate([cos_part] * 4, axis=1),
            np.concatenate([-sin_part, sin_part] * 2, axis=1),
        ]
    ).astype(np.float32)


def per_device(
    ends_in,
    lengths,
    times,
    norm_gain,
    attend_in,
    attend_out,
    time_weight,
    time_bias,
    expand_weight,
    expand_bias,
    reduce_weight,
    reduce_bias,
):
    local = ends_in[0]
    micro = lengths.shape[1]
    assert micro == 2
    width = local.shape[1]
    span = local.shape[0] // micro
    hidden = expand_weight.shape[2]
    count = lax.axis_size("rep")
    section = lax.axis_index("section")
    rank = lax.axis_index("rep")
    core = rank & 1
    steps = jnp.exp(-math.log(10000.0) * jnp.arange(EMB // 2, dtype=F32) / (EMB // 2))
    turn = times.reshape(micro * SEGS, 1).astype(F32) * steps
    embed = jnp.concatenate([jnp.cos(turn), jnp.sin(turn)], axis=1)
    mods = jnp.dot(
        embed, time_weight[0].astype(F32), precision=lax.Precision.HIGHEST
    ) + time_bias.astype(F32)
    fused = width // count % 16 == 0 and TILE % (hidden // count) == 0 and count >= 16
    common = Bag(
        args=(
            lengths[0],
            section.reshape(1),
            mods,
            jnp.asarray(angle_table(span)),
            norm_gain,
            expand_bias,
            reduce_bias,
        ),
        sizes=(span, width, hidden, count),
        tokens=local.shape[0],
        cores=2 if fused else 1,
    )
    weights = Bag(
        win=attend_in[0], wout=attend_out[0], wex=expand_weight[0], wre=reduce_weight[0]
    )
    rows = [(local, slot * span) for slot in range(micro)]
    same = lambda *names: {name: name for name in names}
    whole = same("left", "bg", "pa", "jg")
    run = partial(stage, common=common)
    both = (forward, output, mlp, copy_agrad, attend)
    over = lambda block, route: lax.ppermute(block, "section", route)
    swap = lambda block, bit: exchange(block, "rep", bit)
    a = run(
        "first_0",
        parts=(forward,),
        who=0,
        slot=0,
        loads=dict(xv=rows[0], **weights),
        stores=dict(result="leave"),
        kept=False,
    )
    came_0 = over(a.leave, [(0, 1)])
    b = run(
        "first_1",
        parts=(forward,),
        who=0,
        slot=1,
        loads=dict(xv=rows[1], **weights),
        stores=same("result", "left", "qkv", "probs", "middle", "slope", "branch"),
        after=(a.leave,),
        heads_step=1,
    )
    came_1 = over(b.result, [(0, 1)])
    x = run(
        "second_0",
        parts=both,
        who=1,
        slot=0,
        loads=dict(xv=came_0, dyv=rows[0], **weights),
        stores=dict(whole, result=("ends", 0), leave="leave"),
        after=(b.result,),
    )
    back_0 = over(x.leave, [(1, 0)])
    y = run(
        "second_1",
        parts=both,
        who=1,
        slot=1,
        loads=dict(xv=came_1, dyv=rows[1], **weights),
        stores=dict(whole, result=("ends", span), leave="leave"),
        carried=dict(b, ends=x.ends),
        after=(x.leave,),
    )
    back_1 = over(y.leave, [(1, 0)])
    x = run(
        "back_0",
        parts=both,
        who=0,
        slot=0,
        loads=dict(xv=rows[0], dyv=back_0, **weights),
        stores=dict(whole, leave=("ends", 0)),
        carried=dict(x, ends=y.ends),
        after=(y.leave,),
    )
    if fused:
        side = lambda item: lax.dynamic_index_in_dim(item, 1 - core, 0, keepdims=False)
        lefts = [x.left, y.left, swap(side(x.left), 0), swap(side(y.left), 0)]
        others = [swap(item, 0) for item in (x.bg, x.pa, x.jg)]
        embeds = (embed.T, swap(embed.T, 0))
    gates = mods[SEGS : 2 * SEGS, 2 * width :]
    gates = jnp.where(lengths[0, 1, 0] == span, gates[:1], gates)
    cotan = back_1.astype(F32).reshape(SEGS, -1, width)
    made = (cotan * gates[:, None]).reshape(span, width).astype(BF16)
    bg_1 = jnp.where(section == 0, made, y.bg)
    if fused:
        bg_1_other = swap(bg_1, 0)
    part = run(
        "back_1_mlp",
        parts=(mlp,),
        who=0,
        slot=1,
        loads=dict(
            bg=bg_1,
            wre=weights.wre,
            slope=b.slope,
            wex=weights.wex,
            middle=b.middle,
            dyv=back_1,
            branch=b.branch,
        ),
        stores=same("pa", "middle_grad"),
        carried=y,
    )
    pa_1 = part.pa
    bits = bits_of(count)
    term = partial(term_call, sizes=common.sizes, core=core, rank=rank)
    lines = width // count
    deep = EMB // count
    sizes = (hidden // count, hidden // count + lines + 3 * deep + TAIL_ROWS, 3 * lines + GAIN_ROWS)
    bases = left_bases(width, hidden)

    def last_attend(after):
        return run(
            "back_1_attend",
            parts=(attend,),
            who=0,
            slot=1,
            loads=dict(
                agrad=(pa_1, None, (hidden, width)),
                wout=weights.wout,
                probs=b.probs,
                qkv=b.qkv,
                win=weights.win,
                xv=rows[1],
                middle_grad=part.middle_grad,
            ),
            stores=dict(jg="jg", leave=("ends", span)),
            carried=dict(y, ends=x.ends),
            after=after,
        )

    def pair_of(size, first):
        cut = size // 2 if fused else size // 32 * 16
        one = Chunk("rep", bits, cut, (1,) if fused else ())
        two = Chunk("rep", bits, size - cut, (2,) if fused else ())
        if fused:
            send_1, keep_1, send_2, keep_2 = first
            one.add(keep_1)
            two.add(keep_2)
            return one, two, send_1, send_2
        view = first.reshape((count // 2, 2) + first.shape[1:])
        cut = lambda at: lax.dynamic_index_in_dim(view, at, 1, keepdims=False)
        came = swap(cut(1 - core).astype(BF16), 0)
        for item in (cut(core), came):
            one.add(item)
            two.add(item, one.size)
        return one, two, one.split(1), two.split(2)

    if fused:
        pa_other = swap(pa_1, 0)
        sent = term(
            "term_reduce",
            term_reduce,
            lines=sizes[0],
            base=bases[0],
            rows=hidden // 2,
            lefts=lefts,
            rights=[x.bg, bg_1, others[0], bg_1_other],
            after=(pa_1,),
        )
        r1, r2, send_1, send_2 = pair_of(sizes[0], sent)
        came_r1, came_r2 = swap(send_1, 1), swap(send_2, 2)
        sent = term(
            "term_expand",
            term_expand,
            lines=sizes[1],
            base=bases[1],
            rows=width,
            lefts=lefts,
            rights=[x.pa, pa_1, others[1], pa_other],
            embeds=embeds,
            after=(send_1, send_2),
        )
        last = last_attend((sent[0],))
        came_r1, came_r2, jg_1, *sent = join(came_r1, came_r2, last.jg, *sent)
        jg_other = swap(jg_1, 0)
        e1, e2, send_1, send_2 = pair_of(sizes[1], sent)
        came_e1, came_e2 = swap(send_1, 1), swap(send_2, 2)
        r1.add(came_r1)
        r2.add(came_r2)
        send_1, send_2 = r1.split(2), r2.split(1)
        came_r1, came_r2 = swap(send_1, 2), swap(send_2, 1)
        sent = term(
            "term_attend",
            term_attend,
            lines=sizes[2],
            base=bases[3],
            rows=width // 2,
            lefts=lefts,
            rights=[x.jg, jg_1, others[2], jg_other],
            after=(send_1, send_2),
        )
        came_e1, came_e2, came_r1, came_r2, *sent = join(
            came_e1, came_e2, came_r1, came_r2, *sent
        )
        a1, a2, send_1, send_2 = pair_of(sizes[2], sent)
    else:
        last = last_attend(())
        rights = [(x.bg, bg_1), (x.pa, pa_1), (x.jg, last.jg)]
        totals = plain_pieces((x.left, y.left), rights, embed.T, common.sizes)
        r1, r2, send_1, send_2 = pair_of(sizes[0], totals[0])
        r1.add(swap(send_1, 1))
        r2.add(swap(send_2, 2))
        came_r1, came_r2 = swap(r1.split(2), 2), swap(r2.split(1), 1)
        e1, e2, send_1, send_2 = pair_of(sizes[1], totals[1])
        came_e1, came_e2 = swap(send_1, 1), swap(send_2, 2)
        a1, a2, send_1, send_2 = pair_of(sizes[2], totals[2])
    ends = last.ends
    came_a1, came_a2 = swap(send_1, 1), swap(send_2, 2)
    r1.add(came_r1)
    r2.add(came_r2)
    block_r = jnp.concatenate([r1.split(3), r2.split(3)], axis=-2)
    came_r = swap(block_r, 3)
    e1.add(came_e1)
    e2.add(came_e2)
    send_1, send_2 = e1.split(2), e2.split(1)
    came_e1, came_e2 = swap(send_1, 2), swap(send_2, 1)
    came_a1, came_a2, _, _, _ = join(came_a1, came_a2, send_1, send_2, block_r)
    a1.add(came_a1)
    a2.add(came_a2)
    send_1, send_2 = a1.split(2), a2.split(1)
    came_a1, came_a2 = swap(send_1, 2), swap(send_2, 1)
    came_e1, came_e2, _, _ = join(came_e1, came_e2, send_1, send_2)
    e1.add(came_e1)
    e2.add(came_e2)
    block_e = jnp.concatenate([e1.split(3), e2.split(3)], axis=-2)
    came_e = swap(block_e, 3)
    came_r, _ = join(came_r, block_e)
    r1.add(came_r[..., : r1.size, :])
    r2.add(came_r[..., r1.size :, :])
    came_a1, came_a2, _ = join(came_a1, came_a2, came_r)
    a1.add(came_a1)
    a2.add(came_a2)
    block_a = jnp.concatenate([a1.split(3), a2.split(3)], axis=-2)
    came_a = swap(block_a, 3)
    came_e, _ = join(came_e, block_a)
    e1.add(came_e[..., : e1.size, :])
    e2.add(came_e[..., e1.size :, :])
    a1.add(came_a[..., : a1.size, :])
    a2.add(came_a[..., a1.size :, :])
    for bit in range(4, bits):
        for chunk in (r1, r2, e1, e2, a1, a2):
            chunk.add(swap(chunk.split(bit), bit))
    share_r, share_e, share_a = (
        jnp.concatenate([one.total(), two.total()]) for one, two in ((r1, r2), (e1, e2), (a1, a2))
    )
    tall = hidden // width
    side = lambda item, n, size: jnp.concatenate(
        [item[i * size : (i + 1) * size] for i in range(n)], axis=1
    )
    at_o = tall * lines
    at_t = at_o + lines
    small = share_e[at_t + 3 * deep :]
    flat = lambda item, first, n: lax.dynamic_slice_in_dim(
        item[first : first + n].reshape(-1), rank * (n * width // count), n * width // count
    )
    results = (
        flat(share_a, 3 * lines, 1),
        side(share_a, 3, lines),
        share_e[at_o:at_t],
        side(share_e[at_t:], 3, deep),
        flat(small, 1, 3),
        side(share_e, tall, lines),
        flat(small, 4, tall),
        share_r,
        flat(small, 0, 1),
    )
    return (ends[None],) + tuple(piece[None] for piece in results)


def solution(mesh):
    return jax.shard_map(
        per_device,
        mesh=mesh,
        in_specs=(
            P("section", "rep", None),
            P("rep", None, None),
            P("rep", None, None),
            P("section", None),
            P("section", None, None),
            P("section", None, None),
            P("section", None, None),
            P("section", None),
            P("section", None, None),
            P("section", None),
            P("section", None, None),
            P("section", None),
        ),
        out_specs=(
            P("section", "rep", None),
            P("section", "rep"),
            P("section", "rep", None),
            P("section", "rep", None),
            P("section", "rep", None),
            P("section", "rep"),
            P("section", "rep", None),
            P("section", "rep"),
            P("section", "rep", None),
            P("section", "rep"),
        ),
        check_vma=False,
    )
```

time: 253 us -> 261 us (1.032)
  other arithmetic: 38.1 us -> 22.8 us
  waiting for transfers between devices: 63.7 us -> 75.5 us
  Pallas kernels: 107 us -> 117 us
  starting transfers between devices: 32.4 us -> 24.8 us
  local copies, waits for them, and re-layouts: 7.1 us -> 12.6 us
    ppermute x18 -> x24, waiting for transfers between devices: 42.7 us -> 63.3 us  [exchange(): return lax.ppermute(block, axis, [(i, i ^ 1 << bit) for i in range(count)])]
    convert_element_type x16 -> x11, other arithmetic: 26.3 us -> 11 us  [split(): sum((self.take(term, start, left, bit) for term, left, start in self.terms))]
    pallas_call x8 -> x10, Pallas kernels: 107 us -> 117 us  [the longest x7 93.1 us: stage(): pl.pallas_call(partial(stage_kernel, common.sizes, parts, who, slot, plan...]
    ppermute x4, waiting for transfers between devices: 21 us -> 12.2 us  [per_device(): over = lambda block, route: lax.ppermute(block, 'section', route)]
    ppermute x18 -> x24, starting transfers between devices: 27.2 us -> 19.6 us  [exchange(): return lax.ppermute(block, axis, [(i, i ^ 1 << bit) for i in range(count)])]
    unnamed x38 -> x68, local copies, waits for them, and re-layouts: 3.05 us -> 5.38 us
    add x5 -> x3, other arithmetic: 6.18 us -> 4.61 us  [total(): sum((self.take(term, start, left, None) for term, left, start in self.ter...]
  transfers between devices with their start and end apart: 22 -> 28, of which waited for: 11 -> 11; matrix products, arithmetic and copies ran while one was open for 10% -> 10% of each run, Pallas kernels for 35% -> 41%
where the time goes in v1:
time: 261 us; the launch traced here: 256 us
  Pallas kernels  117 us (45%)
  waiting for transfers between devices  75.5 us (29%)
  starting transfers between devices  24.8 us (10%)
  other arithmetic  22.8 us (9%)
  local copies, waits for them, and re-layouts  12.6 us (5%)
    pallas_call x7, Pallas kernels, stage(): pl.pallas_call(partial(stage_kernel, common.sizes, parts, who, slot, plan...  93.1 us
    ppermute x24, waiting for transfers between devices, exchange(): return lax.ppermute(block, axis, [(i, i ^ 1 << bit) for i in range(count)])  63.3 us
    pallas_call x3, Pallas kernels, term_call(): pl.pallas_call(partial(term_kernel, sizes, body, base, len(after)), out_s...  23.9 us
    ppermute x24, starting transfers between devices, exchange(): return lax.ppermute(block, axis, [(i, i ^ 1 << bit) for i in range(count)])  19.6 us
    ppermute x4, waiting for transfers between devices, per_device(): over = lambda block, route: lax.ppermute(block, 'section', route)  12.2 us
    convert_element_type x11, other arithmetic, split(): sum((self.take(term, start, left, bit) for term, left, start in self.terms))  11 us
    unnamed x68, local copies, waits for them, and re-layouts  5.38 us
  transfers between devices with their start and end apart: 28, of which 11 were waited for; matrix products, arithmetic and copies ran while one was open for 10% of the time, Pallas kernels for 41%

profile of v1, /device:TPU:0, one launch (start us, length us, event | category | flops | bytes accessed | tf_op | source)
XLA Modules:
  0.0 255.8 jit_solution(6140064718719251849)
XLA Ops:
  2.4 1.0 convolution_add_fusion.refs_2_
  3.4 11.2 %first_0.1.refs_12_ = bf16[256,768]{1,0:T(8,128)(2,1)} custom-call(s32[2,4]{1,0:T(2,128)} %bitcast.176, s32[1]{0:T(128)} %bitcast.1.refs_1_, f32[8,2304]{1,0:T(8,128)} %convolution_add_fusion.refs_2_, f32[2,256,128]{2,1,0:T(8,128)} %constant.51.clone.refs_3_, bf16[1,768]{1,0:T(2,128)(2,1)} %refs_4_.13, bf16[1,3072]{1,0:T(2,128)(2,1)} %refs_5_.13, ...), custom_call_target="tpu_custom_call" | custom-call | tf_op jit(solution)/shard_map/first_0/pallas_call | solution.py:698
  14.7 1.3 collective-permute-start.1
  16.0 16.9 %first_1.1 = (bf16[256,768]{1,0:T(8,128)(2,1)}, bf16[2,2688,256]{2,1,0:T(8,128)(2,1)}, bf16[256,2304]{1,0:T(8,128)(2,1)}, f32[12,256,256]{2,1,0:T(8,128)}, f32[2...) custom-call(s32[2,4]{1,0:T(2,128)} %bitcast.177, s32[1]{0:T(128)} %bitcast.1.refs_1_, ...), custom_call_target="tpu_custom_call" | custom-call | tf_op jit(solution)/shard_map/first_1/pallas_call | solution.py:698
  32.9 1.3 collective-permute-start
  36.9 10.4 %second_0.1 = (bf16[2,2688,256]{2,1,0:T(8,128)(2,1)}, bf16[256,768]{1,0:T(8,128)(2,1)}, bf16[272,3840]{1,0:T(8,128)(2,1)}, bf16[272,2304]{1,0:T(8,128)(2,1)}, bf...) custom-call(s32[2,4]{1,0:T(2,128)} %bitcast.178, s32[1]{0:T(128)} %bitcast.1.refs_1_, ...), custom_call_target="tpu_custom_call" | custom-call | tf_op jit(solution)/shard_map/second_0/pallas_call | solution.py:698
  47.3 1.3 collective-permute-start.3
  49.4 7.2 %second_1.1 = (bf16[2,2688,256]{2,1,0:T(8,128)(2,1)}, bf16[256,768]{1,0:T(8,128)(2,1)}, bf16[272,3840]{1,0:T(8,128)(2,1)}, bf16[272,2304]{1,0:T(8,128)(2,1)}, bf...) custom-call(s32[2,4]{1,0:T(2,128)} %bitcast.179, ...), custom_call_target="tpu_custom_call", output_to_operand_aliasing={{0}: (13, {}), {4}: (14, {})} | custom-call | tf_op jit(solution)/shard_map/second_1/pallas_call | solution.py:698
  56.5 1.3 collective-permute-start.2
  58.6 1.4 dynamic-slice_bitcast_fusion
  60.5 10.6 %collective-permute-done.3.refs_8_ = bf16[256,768]{1,0:T(8,128)(2,1)S(1)} collective-permute-done((bf16[256,768]{1,0:T(8,128)(2,1)}, bf16[256,768]{1,0:T(8,128)(2,1)S(1)}, u32[]{:S(2)}, u32[]{:S(2)}) %collective-permute-start.3) | collective-permute-done | bytes 393248 | tf_op jit(solution)/shard_map/ppermute | solution.py:825
  71.9 23.1 %back_0.1 = (bf16[2,2688,256]{2,1,0:T(8,128)(2,1)}, bf16[256,768]{1,0:T(8,128)(2,1)}, bf16[272,3840]{1,0:T(8,128)(2,1)}, bf16[272,2304]{1,0:T(8,128)(2,1)}, bf16[512,768]{1,0:T(8,128)(2,1)}) custom-call(s32[2,4]{1,0:T(2,128)} %bitcast.180, s32[1]{0:T(128)} %bitcast.1.refs_1_, ...), custom_call_target="tpu_custom_call", output_to_operand_aliasing={{0}: (13, {}), {1}: (14, {}), {2}: (15, {}), {3}: (16, {}),... | custom-call | tf_op jit(solution)/shard_map/back_0/pallas_call | solution.py:698
  95.0 1.6 collective-permute-done.2.refs_12_
  97.5 12.3 %back_1_mlp.1 = (bf16[272,3840]{1,0:T(8,128)(2,1)}, f32[256,768]{1,0:T(8,128)}) custom-call(s32[2,4]{1,0:T(2,128)} %bitcast.181, s32[1]{0:T(128)} %bitcast.1.refs_1_, f32[8,2304]{1,0:T(8,128)} %convolution_add_fusion.refs_2_, f32[2,256,128]{2,1,0:T(8,128)} %constant.51.clone.refs_3_, bf16[1,768]{1,0:T(2,128)(2,1)} %refs_4_.13, ...), custom_call_target="tpu_custom_call", output_to_operand_aliasing={{0}: (14, {})} | custom-call | tf_op jit(solution)/shard_map/back_1_mlp/pallas_call | solution.py:698
  110.8 5.8 %collective-permute-done.9.refs_8_ = bf16[256,768]{1,0:T(8,128)(2,1)S(1)} collective-permute-done((bf16[256,768]{1,0:T(8,128)(2,1)S(1)}, bf16[256,768]{1,0:T(8,128)(2,1)S(1)}, u32[]{:S(2)}, u32[]{:S(2)}) %collective-permute-start.9) | collective-permute-done | bytes 393248 | tf_op jit(solution)/shard_map/ppermute | solution.py:752
  116.7 1.6 collective-permute-done.10.refs_9_
  120.0 6.3 %term_reduce.1 = (bf16[4,96,768]{2,1,0:T(8,128)(2,1)}, f32[4,96,768]{2,1,0:T(8,128)}, bf16[4,96,768]{2,1,0:T(8,128)(2,1)}, f32[4,96,768]{2,1,0:T(8,128)}) custom-call(s32[1]{0:T(128)} %bitcast.10.refs_0_, s32[1]{0:T(128)} %bitcast.11.refs_1_, bf16[2,2688,256]{2,1,0:T(8,128)(2,1)} %get-tuple-element.94.refs_2_.refs_4_, ...), custom_call_target="tpu_custom_call" | custom-call | tf_op jit(solution)/shard_map/term_reduce/pallas_call | solution.py:549
  126.3 1.8 collective-permute-start.11
  128.1 1.5 collective-permute-start.12
  129.9 1.2 collective-permute-done.4.refs_3_
  131.8 11.5 %term_expand.1 = (bf16[4,144,768]{2,1,0:T(8,128)(2,1)}, f32[4,144,768]{2,1,0:T(8,128)}, bf16[4,144,768]{2,1,0:T(8,128)(2,1)}, f32[4,144,768]{2,1,0:T(8,128)}) custom-call(s32[1]{0:T(128)} %bitcast.10.refs_0_, s32[1]{0:T(128)} %bitcast.11.refs_1_, f32[128,8]{1,0:T(8,128)} %bitcast.175, f32[128,8]{1,0:T(8,128)} %copy-done.32, ...), custom_call_target="tpu_custom_call" | custom-call | tf_op jit(solution)/shard_map/term_expand/pallas_call | solution.py:549
  143.3 12.1 %back_1_attend.1 = (bf16[272,2304]{1,0:T(8,128)(2,1)}, bf16[512,768]{1,0:T(8,128)(2,1)}) custom-call(s32[2,4]{1,0:T(2,128)} %bitcast.182, s32[1]{0:T(128)} %bitcast.1.refs_1_, f32[8,2304]{1,0:T(8,128)} %convolution_add_fusion.refs_2_, f32[2,256,128]{2,1,0:T(8,128)} %constant.51.clone.refs_3_, ...), custom_call_target="tpu_custom_call", output_to_operand_aliasing={{0}: (14, {}), {1}: (15, {})} | custom-call | tf_op jit(solution)/shard_map/back_1_attend/pallas_call | solution.py:698
  156.4 1.9 collective-permute-start.15
  158.3 1.2 fusion.13.refs_11_
  159.5 1.6 collective-permute-start.16
  161.1 6.0 %term_attend.1 = (bf16[4,80,768]{2,1,0:T(8,128)(2,1)}, f32[4,80,768]{2,1,0:T(8,128)}, bf16[4,80,768]{2,1,0:T(8,128)(2,1)}, f32[4,80,768]{2,1,0:T(8,128)}) custom-call(s32[1]{0:T(128)} %bitcast.10.refs_0_, s32[1]{0:T(128)} %bitcast.11.refs_1_, bf16[2,2688,256]{2,1,0:T(8,128)(2,1)} %get-tuple-element.94.refs_2_.refs_4_, ...), custom_call_target="tpu_custom_call" | custom-call | tf_op jit(solution)/shard_map/term_attend/pallas_call | solution.py:549
  167.2 17.2 %collective-permute-done.15 = bf16[2,96,768]{2,1,0:T(8,128)(2,1)} collective-permute-done((bf16[2,96,768]{2,1,0:T(8,128)(2,1)S(1)}, bf16[2,96,768]{2,1,0:T(8,128)(2,1)}, u32[]{:S(2)}, u32[]{:S(2)}) %collective-permute-start.15) | collective-permute-done | bytes 294944 | tf_op jit(solution)/shard_map/ppermute | solution.py:752
  185.1 1.5 collective-permute-start.19
  187.1 1.2 fusion.2
  188.3 1.6 collective-permute-start.24
  190.0 1.2 fusion.3
  191.7 1.2 fusion.16
  193.0 2.7 %collective-permute-start.23 = (bf16[192,768]{1,0:T(8,128)(2,1)S(1)}, bf16[192,768]{1,0:T(8,128)(2,1)S(1)}, u32[]{:S(2)}, u32[]{:S(2)}) collective-permute-start(bf16[192,768]{1,0:T(8,128)(2,1)S(1)} %pad_maximum_fusion.2), channel_id=1, source_target_pairs={{0,8},{1,9},{2,10},{3,11},{4,12},{5,13},{6,14},{7,15},{8,0},{9,1},... | collective-permute-start | bytes 884744 | tf_op jit(solution)/shard_map/ppermute | solution.py:752
  195.7 3.9 %collective-permute-done.19 = bf16[4,80,768]{2,1,0:T(8,128)(2,1)} collective-permute-done((bf16[4,80,768]{2,1,0:T(8,128)(2,1)}, bf16[4,80,768]{2,1,0:T(8,128)(2,1)}, u32[]{:S(2)}, u32[]{:S(2)}) %collective-permute-start.19) | collective-permute-done | bytes 491552 | tf_op jit(solution)/shard_map/ppermute | solution.py:752
  199.6 7.8 %collective-permute-done.20 = bf16[4,80,768]{2,1,0:T(8,128)(2,1)} collective-permute-done((bf16[4,80,768]{2,1,0:T(8,128)(2,1)}, bf16[4,80,768]{2,1,0:T(8,128)(2,1)}, u32[]{:S(2)}, u32[]{:S(2)}) %collective-permute-start.20) | collective-permute-done | bytes 491552 | tf_op jit(solution)/shard_map/ppermute | solution.py:752
  207.4 1.0 fusion.18
  208.5 1.0 fusion.19
  210.1 6.7 %collective-permute-done.24 = bf16[2,144,768]{2,1,0:T(8,128)(2,1)S(1)} collective-permute-done((bf16[2,144,768]{2,1,0:T(8,128)(2,1)S(1)}, bf16[2,144,768]{2,1,0:T(8,128)(2,1)S(1)}, u32[]{:S(2)}, u32[]{:S(2)}) %collective-permute-start.24) | collective-permute-done | bytes 442400 | tf_op jit(solution)/shard_map/ppermute | solution.py:752
  216.8 1.0 fusion.9
  217.8 1.0 fusion.10
  219.5 1.2 fusion.15
  221.6 1.0 collective-permute-done.21
  222.5 1.1 fusion.21
  225.3 2.1 collective-permute-start.26
  227.4 18.1 %collective-permute-done.27 = bf16[288,768]{1,0:T(8,128)(2,1)S(1)} collective-permute-done((bf16[288,768]{1,0:T(8,128)(2,1)S(1)}, bf16[288,768]{1,0:T(8,128)(2,1)S(1)}, u32[]{:S(2)}, u32[]{:S(2)}) %collective-permute-start.27) | collective-permute-done | bytes 442400 | tf_op jit(solution)/shard_map/ppermute | solution.py:752
  245.5 2.0 fusion.7
  248.3 1.1 fusion.24
  252.7 1.4 fusion.20
  (136 shorter events, 23.2 us)
Async XLA Ops:
  14.7 19.5 %copy-start.33 = (s32[1,2,4]{2,1,0:T(2,128)S(1)}, s32[1,2,4]{2,1,0:T(2,128)}, u32[]{:S(2)}) copy-start(s32[1,2,4]{2,1,0:T(2,128)} %param.14) | copy-start | bytes 100
  14.7 21.5 %collective-permute-start.1 = (bf16[256,768]{1,0:T(8,128)(2,1)}, bf16[256,768]{1,0:T(8,128)(2,1)S(1)}, u32[]{:S(2)}, u32[]{:S(2)}) collective-permute-start(bf16[256,768]{1,0:T(8,128)(2,1)} %first_0.1.refs_12_), channel_id=1, source_target_pairs={{0,16},{1,17},{2,18},{3,19},{4,20},{5,21},{6,22},{7,23},{8,24},{9,... | collective-permute-start | bytes 1179656 | tf_op jit(solution)/shard_map/ppermute | solution.py:825
  32.9 15.7 %collective-permute-start = (bf16[256,768]{1,0:T(8,128)(2,1)}, bf16[256,768]{1,0:T(8,128)(2,1)S(1)}, u32[]{:S(2)}, u32[]{:S(2)}) collective-permute-start(bf16[256,768]{1,0:T(8,128)(2,1)} %get-tuple-element.73.refs_13_), channel_id=1, source_target_pairs={{0,16},{1,17},{2,18},{3,19},{4,20},{5,21},{6,22},{7,23},{8,24},{9,... | collective-permute-start | bytes 1179656 | tf_op jit(solution)/shard_map/ppermute | solution.py:825
  47.3 23.8 %collective-permute-start.3 = (bf16[256,768]{1,0:T(8,128)(2,1)}, bf16[256,768]{1,0:T(8,128)(2,1)S(1)}, u32[]{:S(2)}, u32[]{:S(2)}) collective-permute-start(bf16[256,768]{1,0:T(8,128)(2,1)} %get-tuple-element.76.refs_15_), channel_id=1, source_target_pairs={{16,0},{17,1},{18,2},{19,3},{20,4},{21,5},{22,6},{23,7},{24,8},{25... | collective-permute-start | bytes 1179656 | tf_op jit(solution)/shard_map/ppermute | solution.py:825
  56.5 40.1 %collective-permute-start.2 = (bf16[256,768]{1,0:T(8,128)(2,1)}, bf16[256,768]{1,0:T(8,128)(2,1)S(1)}, u32[]{:S(2)}, u32[]{:S(2)}) collective-permute-start(bf16[256,768]{1,0:T(8,128)(2,1)} %get-tuple-element.77.refs_18_), channel_id=1, source_target_pairs={{16,0},{17,1},{18,2},{19,3},{20,4},{21,5},{22,6},{23,7},{24,8},{25... | collective-permute-start | bytes 1179656 | tf_op jit(solution)/shard_map/ppermute | solution.py:825
  60.0 58.3 %collective-permute-start.6 = (bf16[2688,256]{1,0:T(8,128)(2,1)S(1)}, bf16[2688,256]{1,0:T(8,128)(2,1)S(1)}, u32[]{:S(2)}, u32[]{:S(2)}) collective-permute-start(bf16[2688,256]{1,0:T(8,128)(2,1)S(1)} %dynamic-slice_bitcast_fusion), channel_id=1, source_target_pairs={{0,1},{1,0},{2,3},{3,2},{4,5},{5,4},{6,7},{7,6},{8,9},{9,8},{10,11... | collective-permute-start | bytes 4128776 | tf_op jit(solution)/shard_map/ppermute | solution.py:752
  71.9 24.7 %copy-start.19 = (bf16[256,768]{1,0:T(8,128)(2,1)S(1)}, bf16[256,768]{1,0:T(8,128)(2,1)}, u32[]{:S(2)}) copy-start(bf16[256,768]{1,0:T(8,128)(2,1)} %get-tuple-element.78) | copy-start | bytes 1179652
  95.0 36.3 %collective-permute-start.7 = (bf16[272,3840]{1,0:T(8,128)(2,1)}, bf16[272,3840]{1,0:T(8,128)(2,1)}, u32[]{:S(2)}, u32[]{:S(2)}) collective-permute-start(bf16[272,3840]{1,0:T(8,128)(2,1)} %get-tuple-element.96.refs_8_), channel_id=1, source_target_pairs={{0,1},{1,0},{2,3},{3,2},{4,5},{5,4},{6,7},{7,6},{8,9},{9,8},{10,11... | collective-permute-start | bytes 6266888 | tf_op jit(solution)/shard_map/ppermute | solution.py:752
  97.5 12.4 %copy-start.2 = (bf16[2,2688,256]{2,1,0:T(8,128)(2,1)S(1)}, bf16[2,2688,256]{2,1,0:T(8,128)(2,1)}, u32[]{:S(2)}) copy-start(bf16[2,2688,256]{2,1,0:T(8,128)(2,1)} %get-tuple-element.94.refs_2_.refs_4_) | copy-start | bytes 8257540
  109.8 6.8 %copy-start.6 = (bf16[256,768]{1,0:T(8,128)(2,1)S(1)}, bf16[256,768]{1,0:T(8,128)(2,1)}, u32[]{:S(2)}) copy-start(bf16[256,768]{1,0:T(8,128)(2,1)} %fusion.11.refs_7_) | copy-start | bytes 1179652
  109.8 21.5 %collective-permute-start.8 = (bf16[272,3840]{1,0:T(8,128)(2,1)}, bf16[272,3840]{1,0:T(8,128)(2,1)}, u32[]{:S(2)}, u32[]{:S(2)}) collective-permute-start(bf16[272,3840]{1,0:T(8,128)(2,1)} %get-tuple-element.83.refs_10_.refs_9_.refs_7_), channel_id=1, source_target_pairs={{0,1},{1,0},{2,3},{3,2},{4,5},{5,4},{6,7},{7,6},{8,9},{9,8},{10,11... | collective-permute-start | bytes 6266888 | tf_op jit(solution)/shard_map/ppermute | solution.py:752
  110.0 8.3 %collective-permute-start.5 = (bf16[2688,256]{1,0:T(8,128)(2,1)S(1)}, bf16[2688,256]{1,0:T(8,128)(2,1)S(1)}, u32[]{:S(2)}, u32[]{:S(2)}) collective-permute-start(bf16[2688,256]{1,0:T(8,128)(2,1)S(1)} %dynamic-slice_bitcast_fusion.1), channel_id=1, source_target_pairs={{0,1},{1,0},{2,3},{3,2},{4,5},{5,4},{6,7},{7,6},{8,9},{9,8},{10,11... | collective-permute-start | bytes 4128776 | tf_op jit(solution)/shard_map/ppermute | solution.py:752
  110.8 5.8 %collective-permute-start.9 = (bf16[256,768]{1,0:T(8,128)(2,1)S(1)}, bf16[256,768]{1,0:T(8,128)(2,1)S(1)}, u32[]{:S(2)}, u32[]{:S(2)}) collective-permute-start(bf16[256,768]{1,0:T(8,128)(2,1)S(1)} %copy-done.10), channel_id=1, source_target_pairs={{0,1},{1,0},{2,3},{3,2},{4,5},{5,4},{6,7},{7,6},{8,9},{9,8},{10,11... | collective-permute-start | bytes 1179656 | tf_op jit(solution)/shard_map/ppermute | solution.py:752
  116.6 1.7 collective-permute-start.10
  120.0 11.2 %copy-start.5 = (bf16[272,2304]{1,0:T(8,128)(2,1)S(1)}, bf16[272,2304]{1,0:T(8,128)(2,1)}, u32[]{:S(2)}) copy-start(bf16[272,2304]{1,0:T(8,128)(2,1)} %get-tuple-element.112.refs_6_) | copy-start | bytes 3760132
  126.3 29.0 %collective-permute-start.11 = (bf16[4,96,768]{2,1,0:T(8,128)(2,1)}, bf16[4,96,768]{2,1,0:T(8,128)(2,1)S(1)}, u32[]{:S(2)}, u32[]{:S(2)}) collective-permute-start(bf16[4,96,768]{2,1,0:T(8,128)(2,1)} %get-tuple-element.98.refs_12_), channel_id=1, source_target_pairs={{0,2},{1,3},{2,0},{3,1},{4,6},{5,7},{6,4},{7,5},{8,10},{9,11},{10,... | collective-permute-start | bytes 1769480 | tf_op jit(solution)/shard_map/ppermute | solution.py:752
  128.1 27.2 %collective-permute-start.12 = (bf16[4,96,768]{2,1,0:T(8,128)(2,1)}, bf16[4,96,768]{2,1,0:T(8,128)(2,1)}, u32[]{:S(2)}, u32[]{:S(2)}) collective-permute-start(bf16[4,96,768]{2,1,0:T(8,128)(2,1)} %get-tuple-element.99.refs_13_), channel_id=1, source_target_pairs={{0,4},{1,5},{2,6},{3,7},{4,0},{5,1},{6,2},{7,3},{8,12},{9,13},{10,... | collective-permute-start | bytes 1769480 | tf_op jit(solution)/shard_map/ppermute | solution.py:752
  129.8 1.3 collective-permute-start.4
  131.1 28.4 %collective-permute-start.17 = (bf16[272,2304]{1,0:T(8,128)(2,1)S(1)}, bf16[272,2304]{1,0:T(8,128)(2,1)}, u32[]{:S(2)}, u32[]{:S(2)}) collective-permute-start(bf16[272,2304]{1,0:T(8,128)(2,1)S(1)} %copy-done.5), channel_id=1, source_target_pairs={{0,1},{1,0},{2,3},{3,2},{4,5},{5,4},{6,7},{7,6},{8,9},{9,8},{10,11... | collective-permute-start | bytes 3760136 | tf_op jit(solution)/shard_map/ppermute | solution.py:752
  143.3 13.1 %copy-start.13 = (f32[4,96,768]{2,1,0:T(8,128)S(1)}, f32[4,96,768]{2,1,0:T(8,128)}, u32[]{:S(2)}) copy-start(f32[4,96,768]{2,1,0:T(8,128)} %get-tuple-element.108) | copy-start | bytes 3538948
  155.4 5.7 %copy-start.17 = (bf16[4,96,768]{2,1,0:T(8,128)(2,1)}, bf16[4,96,768]{2,1,0:T(8,128)(2,1)S(1)}, u32[]{:S(2)}) copy-start(bf16[4,96,768]{2,1,0:T(8,128)(2,1)S(1)} %collective-permute-done.11) | copy-start | bytes 1769476
  155.4 5.7 %collective-permute-start.18 = (bf16[272,2304]{1,0:T(8,128)(2,1)}, bf16[272,2304]{1,0:T(8,128)(2,1)}, u32[]{:S(2)}, u32[]{:S(2)}) collective-permute-start(bf16[272,2304]{1,0:T(8,128)(2,1)} %get-tuple-element.113.refs_7_), channel_id=1, source_target_pairs={{0,1},{1,0},{2,3},{3,2},{4,5},{5,4},{6,7},{7,6},{8,9},{9,8},{10,11... | collective-permute-start | bytes 3760136 | tf_op jit(solution)/shard_map/ppermute | solution.py:752
  155.6 29.5 %collective-permute-start.13 = (bf16[4,144,768]{2,1,0:T(8,128)(2,1)}, bf16[4,144,768]{2,1,0:T(8,128)(2,1)}, u32[]{:S(2)}, u32[]{:S(2)}) collective-permute-start(bf16[4,144,768]{2,1,0:T(8,128)(2,1)} %get-tuple-element.106.refs_16_), channel_id=1, source_target_pairs={{0,2},{1,3},{2,0},{3,1},{4,6},{5,7},{6,4},{7,5},{8,10},{9,11},{10,... | collective-permute-start | bytes 2654216 | tf_op jit(solution)/shard_map/ppermute | solution.py:752
  156.1 29.0 %collective-permute-start.14 = (bf16[4,144,768]{2,1,0:T(8,128)(2,1)}, bf16[4,144,768]{2,1,0:T(8,128)(2,1)}, u32[]{:S(2)}, u32[]{:S(2)}) collective-permute-start(bf16[4,144,768]{2,1,0:T(8,128)(2,1)} %get-tuple-element.107), channel_id=1, source_target_pairs={{0,4},{1,5},{2,6},{3,7},{4,0},{5,1},{6,2},{7,3},{8,12},{9,13},{10,... | collective-permute-start | bytes 2654216 | tf_op jit(solution)/shard_map/ppermute | solution.py:752
  156.4 4.7 %copy-start.11 = (bf16[2,96,768]{2,1,0:T(8,128)(2,1)}, bf16[2,96,768]{2,1,0:T(8,128)(2,1)S(1)}, u32[]{:S(2)}) copy-start(bf16[2,96,768]{2,1,0:T(8,128)(2,1)S(1)} %fusion.12.refs_10_) | copy-start | bytes 884740
  156.4 28.0 %collective-permute-start.15 = (bf16[2,96,768]{2,1,0:T(8,128)(2,1)S(1)}, bf16[2,96,768]{2,1,0:T(8,128)(2,1)}, u32[]{:S(2)}, u32[]{:S(2)}) collective-permute-start(bf16[2,96,768]{2,1,0:T(8,128)(2,1)S(1)} %fusion.12.refs_10_), channel_id=1, source_target_pairs={{0,4},{1,5},{2,6},{3,7},{4,0},{5,1},{6,2},{7,3},{8,12},{9,13},{10,... | collective-permute-start | bytes 884744 | tf_op jit(solution)/shard_map/ppermute | solution.py:752
  159.5 27.6 %copy-start.7 = (f32[4,144,768]{2,1,0:T(8,128)S(1)}, f32[4,144,768]{2,1,0:T(8,128)}, u32[]{:S(2)}) copy-start(f32[4,144,768]{2,1,0:T(8,128)} %get-tuple-element.121) | copy-start | bytes 5308420
  159.5 24.9 %collective-permute-start.16 = (bf16[2,96,768]{2,1,0:T(8,128)(2,1)S(1)}, bf16[2,96,768]{2,1,0:T(8,128)(2,1)S(1)}, u32[]{:S(2)}, u32[]{:S(2)}) collective-permute-start(bf16[2,96,768]{2,1,0:T(8,128)(2,1)S(1)} %fusion.13.refs_11_), channel_id=1, source_target_pairs={{0,2},{1,3},{2,0},{3,1},{4,6},{5,7},{6,4},{7,5},{8,10},{9,11},{10,... | collective-permute-start | bytes 884744 | tf_op jit(solution)/shard_map/ppermute | solution.py:752
  167.1 22.8 %copy-start.8 = (f32[4,144,768]{2,1,0:T(8,128)S(1)}, f32[4,144,768]{2,1,0:T(8,128)}, u32[]{:S(2)}) copy-start(f32[4,144,768]{2,1,0:T(8,128)} %get-tuple-element.123) | copy-start | bytes 5308420
  185.1 14.5 %collective-permute-start.19 = (bf16[4,80,768]{2,1,0:T(8,128)(2,1)}, bf16[4,80,768]{2,1,0:T(8,128)(2,1)}, u32[]{:S(2)}, u32[]{:S(2)}) collective-permute-start(bf16[4,80,768]{2,1,0:T(8,128)(2,1)} %get-tuple-element.119), channel_id=1, source_target_pairs={{0,2},{1,3},{2,0},{3,1},{4,6},{5,7},{6,4},{7,5},{8,10},{9,11},{10,... | collective-permute-start | bytes 1474568 | tf_op jit(solution)/shard_map/ppermute | solution.py:752
  186.6 20.8 %collective-permute-start.20 = (bf16[4,80,768]{2,1,0:T(8,128)(2,1)}, bf16[4,80,768]{2,1,0:T(8,128)(2,1)}, u32[]{:S(2)}, u32[]{:S(2)}) collective-permute-start(bf16[4,80,768]{2,1,0:T(8,128)(2,1)} %get-tuple-element.120), channel_id=1, source_target_pairs={{0,4},{1,5},{2,6},{3,7},{4,0},{5,1},{6,2},{7,3},{8,12},{9,13},{10,... | collective-permute-start | bytes 1474568 | tf_op jit(solution)/shard_map/ppermute | solution.py:752
  187.1 4.6 %copy-start.14 = (f32[4,96,768]{2,1,0:T(8,128)S(1)}, f32[4,96,768]{2,1,0:T(8,128)}, u32[]{:S(2)}) copy-start(f32[4,96,768]{2,1,0:T(8,128)} %get-tuple-element.108) | copy-start | bytes 3538948
  187.1 4.6 %copy-start.18 = (bf16[4,96,768]{2,1,0:T(8,128)(2,1)S(1)}, bf16[4,96,768]{2,1,0:T(8,128)(2,1)}, u32[]{:S(2)}) copy-start(bf16[4,96,768]{2,1,0:T(8,128)(2,1)} %copy-done.17) | copy-start | bytes 1769476
  188.3 28.5 %collective-permute-start.24 = (bf16[2,144,768]{2,1,0:T(8,128)(2,1)S(1)}, bf16[2,144,768]{2,1,0:T(8,128)(2,1)S(1)}, u32[]{:S(2)}, u32[]{:S(2)}) collective-permute-start(bf16[2,144,768]{2,1,0:T(8,128)(2,1)S(1)} %fusion.2), channel_id=1, source_target_pairs={{0,4},{1,5},{2,6},{3,7},{4,0},{5,1},{6,2},{7,3},{8,12},{9,13},{10,... | collective-permute-start | bytes 1327112 | tf_op jit(solution)/shard_map/ppermute | solution.py:752
  189.9 17.5 %copy-start.15 = (f32[4,80,768]{2,1,0:T(8,128)S(1)}, f32[4,80,768]{2,1,0:T(8,128)}, u32[]{:S(2)}) copy-start(f32[4,80,768]{2,1,0:T(8,128)} %get-tuple-element.128) | copy-start | bytes 2949124
  191.1 17.3 %copy-start.16 = (f32[4,80,768]{2,1,0:T(8,128)S(1)}, f32[4,80,768]{2,1,0:T(8,128)}, u32[]{:S(2)}) copy-start(f32[4,80,768]{2,1,0:T(8,128)} %get-tuple-element.118) | copy-start | bytes 2949124
  191.1 25.6 %collective-permute-start.25 = (bf16[2,144,768]{2,1,0:T(8,128)(2,1)S(1)}, bf16[2,144,768]{2,1,0:T(8,128)(2,1)S(1)}, u32[]{:S(2)}, u32[]{:S(2)}) collective-permute-start(bf16[2,144,768]{2,1,0:T(8,128)(2,1)S(1)} %fusion.3), channel_id=1, source_target_pairs={{0,2},{1,3},{2,0},{3,1},{4,6},{5,7},{6,4},{7,5},{8,10},{9,11},{10,... | collective-permute-start | bytes 1327112 | tf_op jit(solution)/shard_map/ppermute | solution.py:752
  193.0 26.5 %collective-permute-start.23 = (bf16[192,768]{1,0:T(8,128)(2,1)S(1)}, bf16[192,768]{1,0:T(8,128)(2,1)S(1)}, u32[]{:S(2)}, u32[]{:S(2)}) collective-permute-start(bf16[192,768]{1,0:T(8,128)(2,1)S(1)} %pad_maximum_fusion.2), channel_id=1, source_target_pairs={{0,8},{1,9},{2,10},{3,11},{4,12},{5,13},{6,14},{7,15},{8,0},{9,1},... | collective-permute-start | bytes 884744 | tf_op jit(solution)/shard_map/ppermute | solution.py:752
  208.4 14.1 %collective-permute-start.21 = (bf16[2,80,768]{2,1,0:T(8,128)(2,1)S(1)}, bf16[2,80,768]{2,1,0:T(8,128)(2,1)S(1)}, u32[]{:S(2)}, u32[]{:S(2)}) collective-permute-start(bf16[2,80,768]{2,1,0:T(8,128)(2,1)S(1)} %fusion.18), channel_id=1, source_target_pairs={{0,4},{1,5},{2,6},{3,7},{4,0},{5,1},{6,2},{7,3},{8,12},{9,13},{10,... | collective-permute-start | bytes 737288 | tf_op jit(solution)/shard_map/ppermute | solution.py:752
  209.5 10.0 %copy-start.26 = (bf16[2,96,768]{2,1,0:T(8,128)(2,1)S(1)}, bf16[2,96,768]{2,1,0:T(8,128)(2,1)}, u32[]{:S(2)}) copy-start(bf16[2,96,768]{2,1,0:T(8,128)(2,1)} %copy-done.25) | copy-start | bytes 884740
  209.5 13.0 %collective-permute-start.22 = (bf16[2,80,768]{2,1,0:T(8,128)(2,1)S(1)}, bf16[2,80,768]{2,1,0:T(8,128)(2,1)S(1)}, u32[]{:S(2)}, u32[]{:S(2)}) collective-permute-start(bf16[2,80,768]{2,1,0:T(8,128)(2,1)S(1)} %fusion.19), channel_id=1, source_target_pairs={{0,2},{1,3},{2,0},{3,1},{4,6},{5,7},{6,4},{7,5},{8,10},{9,11},{10,... | collective-permute-start | bytes 737288 | tf_op jit(solution)/shard_map/ppermute | solution.py:752
  218.9 26.6 %collective-permute-start.27 = (bf16[288,768]{1,0:T(8,128)(2,1)S(1)}, bf16[288,768]{1,0:T(8,128)(2,1)S(1)}, u32[]{:S(2)}, u32[]{:S(2)}) collective-permute-start(bf16[288,768]{1,0:T(8,128)(2,1)S(1)} %pad_maximum_fusion.1), channel_id=1, source_target_pairs={{0,8},{1,9},{2,10},{3,11},{4,12},{5,13},{6,14},{7,15},{8,0},{9,1},... | collective-permute-start | bytes 1327112 | tf_op jit(solution)/shard_map/ppermute | solution.py:752
  222.5 25.0 %copy-start.28 = (bf16[2,80,768]{2,1,0:T(8,128)(2,1)}, bf16[2,80,768]{2,1,0:T(8,128)(2,1)S(1)}, u32[]{:S(2)}) copy-start(bf16[2,80,768]{2,1,0:T(8,128)(2,1)S(1)} %collective-permute-done.21) | copy-start | bytes 737284
  222.5 25.0 %copy-start.30 = (bf16[2,80,768]{2,1,0:T(8,128)(2,1)}, bf16[2,80,768]{2,1,0:T(8,128)(2,1)S(1)}, u32[]{:S(2)}) copy-start(bf16[2,80,768]{2,1,0:T(8,128)(2,1)S(1)} %collective-permute-done.22) | copy-start | bytes 737284
  225.3 27.4 %collective-permute-start.26 = (bf16[160,768]{1,0:T(8,128)(2,1)}, bf16[160,768]{1,0:T(8,128)(2,1)}, u32[]{:S(2)}, u32[]{:S(2)}) collective-permute-start(bf16[160,768]{1,0:T(8,128)(2,1)} %pad_maximum_fusion.3), channel_id=1, source_target_pairs={{0,8},{1,9},{2,10},{3,11},{4,12},{5,13},{6,14},{7,15},{8,0},{9,1},... | collective-permute-start | bytes 737288 | tf_op jit(solution)/shard_map/ppermute | solution.py:752
  247.5 5.2 %copy-start.29 = (bf16[2,80,768]{2,1,0:T(8,128)(2,1)S(1)}, bf16[2,80,768]{2,1,0:T(8,128)(2,1)}, u32[]{:S(2)}) copy-start(bf16[2,80,768]{2,1,0:T(8,128)(2,1)} %copy-done.28) | copy-start | bytes 737284
  247.5 5.2 %copy-start.31 = (bf16[2,80,768]{2,1,0:T(8,128)(2,1)S(1)}, bf16[2,80,768]{2,1,0:T(8,128)(2,1)}, u32[]{:S(2)}) copy-start(bf16[2,80,768]{2,1,0:T(8,128)(2,1)} %copy-done.30) | copy-start | bytes 737284
  252.1 3.5 %copy-start.1 = (bf16[1,128,2304]{2,1,0:T(8,128)(2,1)S(1)}, bf16[1,128,2304]{2,1,0:T(8,128)(2,1)}, u32[]{:S(2)}) copy-start(bf16[1,128,2304]{2,1,0:T(8,128)(2,1)} %param.19) | copy-start | bytes 1769476
  (14 other events, 15.8 us)
